TPU v7x, 512 devices: a whole 4x4x16 slice. The times are simulated.
512 devices in a mesh: dp: 64 (over y, z_lo, x), head: 8 (over z_hi, core).
Axes of the slice: x: 4, y: 4, z: 16 (z_hi: 4, z_lo: 4; z = z_hi * 4 + z_lo), core: 2. Of those that a mesh axis runs over, the one named last changes fastest.
Arguments:
- response_q: bfloat16 [16384, 5120], P(('dp', 'head')), may hold values from -90 to 90
- response_k: bfloat16 [16384, 1024], P(('dp', 'head')), may hold values from -4.5 to 4.5
- response_saved_values: bfloat16 [16384, 1024], P(('dp', 'head')), may hold values from -4.5 to 4.5
- response_o: bfloat16 [16384, 5120], P(('dp', 'head')), may hold values from -4.5 to 4.5
- response_do: bfloat16 [16384, 5120], P(('dp', 'head')), may hold values from -4.5 to 4.5
- prompt_q: bfloat16 [4096, 5120], P(('dp', 'head')), may hold values from -90 to 90
- prompt_k: bfloat16 [4096, 1024], P(('dp', 'head')), may hold values from -4.5 to 4.5
- prompt_saved_values: bfloat16 [4096, 1024], P(('dp', 'head')), may hold values from -4.5 to 4.5
- prompt_o: bfloat16 [4096, 5120], P(('dp', 'head')), may hold values from -4.5 to 4.5
- prompt_do: bfloat16 [4096, 5120], P(('dp', 'head')), may hold values from -4.5 to 4.5
- resp_len: int32 [256], replicated, may hold values from 4 to 64, as said below
- resp_prompt: int32 [256], replicated, may hold values from 0 to 15, as said below
- plan_rank: int32 [256], replicated, may hold values from 0 to 63, as said below
- plan_offset: int32 [256], replicated, may hold values from 0 to 192, as said below
Outputs:
- response_dq: bfloat16 [16384, 5120], P(('dp', 'head'))
- response_dk: bfloat16 [16384, 1024], P(('dp', 'head'))
- response_dv: bfloat16 [16384, 1024], P(('dp', 'head'))
- prompt_dq: bfloat16 [4096, 5120], P(('dp', 'head'))
- prompt_dk: bfloat16 [4096, 1024], P(('dp', 'head'))
- prompt_dv: bfloat16 [4096, 1024], P(('dp', 'head'))
Inputs may be any that keep to these rules, and one draw needn't show every extreme that they name: `resp_len`: some response has exactly 64 tokens. `resp_prompt`: each prompt has 16 responses. `plan_rank`: each index of dp holds exactly four responses: two of one prompt and two of another. `plan_offset`: the responses of one index of dp fill its rows from row 0 one after another without gaps, in any order; some index of dp holds four responses of 64 tokens.
All inputs are finite; a program needn't handle non-finite values.
Results may differ from a plain program's by a relative error of at most 0.005.
Values may be sent and summed in bfloat16 or wider, within the bound.
A program may use at most 64 MiB of HBM per device.

v0:
```python
import jax
import jax.numpy as jnp
from jax import lax
from jax.sharding import PartitionSpec as P

HEAD_SIZE = 128
QUERY_PER_KV = 5
PROMPT_LENGTH = 256


MASKED_SCORE = -1e30


def row_tables(resp_len, resp_prompt, plan_rank, plan_offset, device, count_of_rows):
    row_ids = jnp.arange(count_of_rows, dtype=jnp.int32)
    holding = plan_rank == device
    member = (
        holding[None, :]
        & (row_ids[:, None] >= plan_offset[None, :])
        & (row_ids[:, None] < (plan_offset + resp_len)[None, :])
    )
    labels = jnp.arange(1, resp_len.shape[0] + 1, dtype=jnp.int32)
    segment = jnp.sum(jnp.where(member, labels[None, :], 0), axis=1)
    owners = jnp.sum(jnp.where(member, resp_prompt[None, :], 0), axis=1)
    first_prompt = jnp.min(jnp.where(holding, resp_prompt, resp_prompt.shape[0]))
    last_prompt = jnp.max(jnp.where(holding, resp_prompt, 0))
    return (segment, owners, first_prompt, last_prompt)


def response_allowed(segment, owners, first_prompt, last_prompt):
    item_count = segment.shape[0]
    row_ids = jnp.arange(item_count, dtype=jnp.int32)
    filled = segment > 0
    take_first = (owners == first_prompt) & filled
    take_last = (owners == last_prompt) & (last_prompt != first_prompt) & filled
    prefix = jnp.concatenate(
        [
            jnp.broadcast_to(take_first[:, None], (item_count, PROMPT_LENGTH)),
            jnp.broadcast_to(take_last[:, None], (item_count, PROMPT_LENGTH)),
        ],
        axis=1,
    )
    own_rows = (
        (segment[:, None] == segment[None, :])
        & filled[:, None]
        & (row_ids[None, :] <= row_ids[:, None])
    )
    return jnp.concatenate([prefix, own_rows], axis=1)


def head_delta(attention_output, output_gradient):
    item_count = attention_output.shape[0]
    heads = attention_output.shape[1] // HEAD_SIZE
    product = (attention_output.astype(jnp.float32) * output_gradient.astype(jnp.float32)).reshape(
        item_count, heads, HEAD_SIZE
    )
    return jnp.sum(product, axis=2).T


def head_grads(
    query_block, output_gradient, deltas, key_row_block, value_row_block, allowed, scale
):
    scores = (
        jnp.einsum("qd,kd->qk", query_block, key_row_block, preferred_element_type=jnp.float32)
        * scale
    )
    masked = jnp.where(allowed, scores, MASKED_SCORE)
    highest = jnp.max(masked, axis=1, keepdims=True)
    totals = jnp.sum(jnp.where(allowed, jnp.exp(masked - highest), 0.0), axis=1, keepdims=True)
    empty_row = jnp.where(jnp.any(allowed, axis=1, keepdims=True), 0.0, 1.0)
    log_total = highest + jnp.log(totals + empty_row)
    likely = jnp.where(allowed, jnp.exp(scores - log_total), 0.0)
    weights = likely.astype(jnp.bfloat16)
    prob_grad = jnp.einsum(
        "qd,kd->qk", output_gradient, value_row_block, preferred_element_type=jnp.float32
    )
    score_grad = (likely * (prob_grad - deltas[:, None])).astype(jnp.bfloat16)
    query_gradient = (
        jnp.einsum("qk,kd->qd", score_grad, key_row_block, preferred_element_type=jnp.float32)
        * scale
    )
    key_gradient = (
        jnp.einsum("qk,qd->kd", score_grad, query_block, preferred_element_type=jnp.float32) * scale
    )
    value_gradient = jnp.einsum(
        "qk,qd->kd", weights, output_gradient, preferred_element_type=jnp.float32
    )
    return (query_gradient, key_gradient, value_gradient)


def group_grads(query_cols, grad_cols, deltas, key_row_block, value_row_block, allowed, scale):
    item_count = query_cols.shape[0]
    count_of_keys = key_row_block.shape[0]

    def advance(carried, query_head):
        query_all, key_sum, value_sum = carried
        column_start = query_head * HEAD_SIZE
        query_one = lax.dynamic_slice_in_dim(query_cols, column_start, HEAD_SIZE, 1)
        grad_one = lax.dynamic_slice_in_dim(grad_cols, column_start, HEAD_SIZE, 1)
        delta_one = lax.dynamic_index_in_dim(deltas, query_head, 0, keepdims=False)
        query_gradient, key_gradient, value_gradient = head_grads(
            query_one, grad_one, delta_one, key_row_block, value_row_block, allowed, scale
        )
        query_all = lax.dynamic_update_slice_in_dim(
            query_all, query_gradient.astype(jnp.bfloat16), column_start, 1
        )
        return ((query_all, key_sum + key_gradient, value_sum + value_gradient), None)

    start_state = (
        jnp.zeros((item_count, QUERY_PER_KV * HEAD_SIZE), jnp.bfloat16),
        jnp.zeros((count_of_keys, HEAD_SIZE), jnp.float32),
        jnp.zeros((count_of_keys, HEAD_SIZE), jnp.float32),
    )
    finished, _ = lax.scan(advance, start_state, jnp.arange(QUERY_PER_KV, dtype=jnp.int32))
    return finished


def all_groups(query_cols, grad_cols, deltas, key_row_block, value_row_block, allowed):
    scale = HEAD_SIZE ** (-0.5)
    query_gradient, key_gradient, value_gradient = group_grads(
        query_cols, grad_cols, deltas, key_row_block, value_row_block, allowed, scale
    )
    return (query_gradient, key_gradient, value_gradient)


def add_at(partial_value, piece, start):
    before = lax.dynamic_slice_in_dim(partial_value, start, piece.shape[0], 0)
    return lax.dynamic_update_slice_in_dim(partial_value, before + piece, start, 0)


def local(
    response_q,
    response_k,
    response_saved_values,
    response_o,
    response_do,
    prompt_q,
    prompt_k,
    prompt_saved_values,
    prompt_o,
    prompt_do,
    resp_len,
    resp_prompt,
    plan_rank,
    plan_offset,
):
    rows_q, rows_k, rows_v, rows_out, rows_grad, lead_q, lead_k, lead_v, lead_out, lead_grad = (
        lax.all_to_all(response_q, "head", split_axis=1, concat_axis=0, tiled=True),
        lax.all_to_all(response_k, "head", split_axis=1, concat_axis=0, tiled=True),
        lax.all_to_all(response_saved_values, "head", split_axis=1, concat_axis=0, tiled=True),
        lax.all_to_all(response_o, "head", split_axis=1, concat_axis=0, tiled=True),
        lax.all_to_all(response_do, "head", split_axis=1, concat_axis=0, tiled=True),
        lax.all_to_all(prompt_q, "head", split_axis=1, concat_axis=0, tiled=True),
        lax.all_to_all(prompt_k, "head", split_axis=1, concat_axis=0, tiled=True),
        lax.all_to_all(prompt_saved_values, "head", split_axis=1, concat_axis=0, tiled=True),
        lax.all_to_all(prompt_o, "head", split_axis=1, concat_axis=0, tiled=True),
        lax.all_to_all(prompt_do, "head", split_axis=1, concat_axis=0, tiled=True),
    )
    rows_delta = head_delta(rows_out, rows_grad)
    lead_delta = head_delta(lead_out, lead_grad)
    device = lax.axis_index("dp")
    count_of_rows = rows_q.shape[0]
    segment, owners, first_prompt, last_prompt = row_tables(
        resp_len, resp_prompt, plan_rank, plan_offset, device, count_of_rows
    )
    whole_k, whole_v = (
        lax.all_gather(lead_k, "dp", axis=0, tiled=True),
        lax.all_gather(lead_v, "dp", axis=0, tiled=True),
    )
    first_start = first_prompt * PROMPT_LENGTH
    last_start = last_prompt * PROMPT_LENGTH
    key_row_block = jnp.concatenate(
        [
            lax.dynamic_slice_in_dim(whole_k, first_start, PROMPT_LENGTH, 0),
            lax.dynamic_slice_in_dim(whole_k, last_start, PROMPT_LENGTH, 0),
            rows_k,
        ],
        axis=0,
    )
    value_row_block = jnp.concatenate(
        [
            lax.dynamic_slice_in_dim(whole_v, first_start, PROMPT_LENGTH, 0),
            lax.dynamic_slice_in_dim(whole_v, last_start, PROMPT_LENGTH, 0),
            rows_v,
        ],
        axis=0,
    )
    allowed = response_allowed(segment, owners, first_prompt, last_prompt)
    rows_dq, rows_dk, rows_dv = all_groups(
        rows_q, rows_grad, rows_delta, key_row_block, value_row_block, allowed
    )
    own_prompt = device // 4
    quarter = device % 4
    quarter_rows = lead_q.shape[0]
    own_start = own_prompt * PROMPT_LENGTH
    own_k = lax.dynamic_slice_in_dim(whole_k, own_start, PROMPT_LENGTH, 0)
    own_v = lax.dynamic_slice_in_dim(whole_v, own_start, PROMPT_LENGTH, 0)
    query_pos = quarter * quarter_rows + jnp.arange(quarter_rows, dtype=jnp.int32)
    causal = jnp.arange(PROMPT_LENGTH, dtype=jnp.int32)[None, :] <= query_pos[:, None]
    lead_dq, lead_dk, lead_dv = all_groups(lead_q, lead_grad, lead_delta, own_k, own_v, causal)
    zero_rows = jnp.zeros(whole_k.shape, jnp.float32)
    partial_key = add_at(
        add_at(
            add_at(zero_rows, rows_dk[:PROMPT_LENGTH], first_start),
            rows_dk[PROMPT_LENGTH : 2 * PROMPT_LENGTH],
            last_start,
        ),
        lead_dk,
        own_start,
    )
    partial_value = add_at(
        add_at(
            add_at(zero_rows, rows_dv[:PROMPT_LENGTH], first_start),
            rows_dv[PROMPT_LENGTH : 2 * PROMPT_LENGTH],
            last_start,
        ),
        lead_dv,
        own_start,
    )
    summed_key, summed_value = (
        lax.psum_scatter(partial_key, "dp", scatter_dimension=0, tiled=True),
        lax.psum_scatter(partial_value, "dp", scatter_dimension=0, tiled=True),
    )
    return (
        lax.all_to_all(rows_dq, "head", split_axis=0, concat_axis=1, tiled=True),
        lax.all_to_all(
            rows_dk[2 * PROMPT_LENGTH :].astype(jnp.bfloat16),
            "head",
            split_axis=0,
            concat_axis=1,
            tiled=True,
        ),
        lax.all_to_all(
            rows_dv[2 * PROMPT_LENGTH :].astype(jnp.bfloat16),
            "head",
            split_axis=0,
            concat_axis=1,
            tiled=True,
        ),
        lax.all_to_all(lead_dq, "head", split_axis=0, concat_axis=1, tiled=True),
        lax.all_to_all(
            summed_key.astype(jnp.bfloat16), "head", split_axis=0, concat_axis=1, tiled=True
        ),
        lax.all_to_all(
            summed_value.astype(jnp.bfloat16), "head", split_axis=0, concat_axis=1, tiled=True
        ),
    )


def solution(mesh):
    in_specs = (
        P(("dp", "head"), None),
        P(("dp", "head"), None),
        P(("dp", "head"), None),
        P(("dp", "head"), None),
        P(("dp", "head"), None),
        P(("dp", "head"), None),
        P(("dp", "head"), None),
        P(("dp", "head"), None),
        P(("dp", "head"), None),
        P(("dp", "head"), None),
        P(),
        P(),
        P(),
        P(),
    )
    out_specs = (
        P(("dp", "head"), None),
        P(("dp", "head"), None),
        P(("dp", "head"), None),
        P(("dp", "head"), None),
        P(("dp", "head"), None),
        P(("dp", "head"), None),
    )
    return jax.shard_map(local, mesh=mesh, in_specs=in_specs, out_specs=out_specs, check_vma=False)
```

profile of v0, /device:TPU:1, one launch (start us, length us, event | category | flops | bytes accessed | tf_op | source)
XLA Modules:
  0.0 1640.9 jit_solution(3434504898575448211)
XLA Ops:
  7.2 28.7 %all_to_all.292 = bf16[8,8,128]{2,0,1:T(8,128)(2,1)} all-to-all(bf16[8,8,128]{2,0,1:T(8,128)(2,1)} %bitcast.158), channel_id=1, replica_groups=mesh['dp'=64,'head'=8] {'head'}, dimensions={1} | all-to-all | bytes 32768 | tf_op jit(solution)/shard_map/all_to_all | solution.py:154
  36.0 4.0 all-to-all-start.4
  39.9 0.6 copy_bitcast_fusion.6
  40.6 11.3 all-to-all-done.4
  51.9 4.0 all-to-all-start.2
  55.8 0.7 all-gather.3.cloned.1.call-update
  56.6 0.9 copy_bitcast_fusion.5
  57.4 10.8 all-to-all-done.2
  68.2 16.3 all_to_all.293
  84.5 18.3 %all_to_all.294 = bf16[8,8,640]{2,0,1:T(8,128)(2,1)S(1)} all-to-all(bf16[8,8,640]{2,0,1:T(8,128)(2,1)} %bitcast.151), channel_id=1, replica_groups=mesh['dp'=64,'head'=8] {'head'}, dimensions={1} | all-to-all | bytes 163840 | tf_op jit(solution)/shard_map/all_to_all | solution.py:157
  102.9 4.7 all-to-all-start.12
  107.6 1.7 copy.79
  109.3 11.8 all-to-all-done.12
  121.1 4.8 all-to-all-start.3
  126.0 0.7 copy.78
  126.8 0.6 select_reduce_fusion.4
  127.6 14.5 all-to-all-done.3
  142.1 9.2 all-to-all-start.6
  153.9 0.8 copy.80
  154.9 0.7 compare_and_fusion
  155.6 0.7 and_and_fusion
  157.1 11.2 all-to-all-done.6
  168.3 11.2 all-to-all-start
  179.8 0.9 bitcast_multiply_fusion
  180.8 1.2 mul.69
  182.4 191.0 %all-gather.3.cloned.1.call-done = bf16[4096,128]{1,0:T(8,128)(2,1)} async-done(((bf16[64,128]{1,0:T(8,128)(2,1)}), bf16[4096,128]{1,0:T(8,128)(2,1)}) %all-gather.3.cloned.1.call-update) | async-done | bytes 1048592 | tf_op jit(solution)/shard_map/all_gather | solution.py:167
  373.4 0.9 constant_dynamic-slice_fusion.3
  374.3 358.1 %all-gather.5.cloned.1.call-done = bf16[4096,128]{1,0:T(8,128)(2,1)} async-done(((bf16[64,128]{1,0:T(8,128)(2,1)}), bf16[4096,128]{1,0:T(8,128)(2,1)}) %all-gather.5.cloned.1.call-update) | async-done | bytes 1048592 | tf_op jit(solution)/shard_map/all_gather | solution.py:168
  732.4 1.5 constant_dynamic-slice_fusion.2
  734.0 54.9 %all-to-all-start.10 = ((bf16[8,8,640]{2,0,1:T(8,128)(2,1)}), bf16[8,8,640]{2,0,1:T(8,128)(2,1)S(1)}, u32[]{:S(2)}, u32[]{:S(2)}) async-start(bf16[8,8,640]{2,0,1:T(8,128)(2,1)} %bitcast.153), calls=%async_computation.10 | async-start | bytes 163840 | tf_op jit(solution)/shard_map/all_to_all | solution.py:153
  788.9 0.8 broadcast_in_dim.104
  789.7 30.6 %while.32 = (s32[]{:T(128)}, bf16[256,640]{1,0:T(8,128)(2,1)}, f32[768,128]{1,0:T(8,128)S(1)}, f32[768,128]{1,0:T(8,128)S(1)}, s32[5]{0:T(128)S(1)}, /*index=5*/...) while((s32[]{:T(128)}, bf16[256,640]{1,0:T(8,128)(2,1)}, ...), condition=%wide.region_11.12_spmd.clone, body=%wide.region_8.11_spmd.clone.sunk | while | flops 255164672 | bytes 7613980 | solution.py:114
  794.9 0.9 fusion.104
  801.0 0.9 fusion.104
  807.2 0.9 fusion.104
  813.3 0.9 fusion.104
  819.4 0.9 fusion.104
  820.3 1.4 broadcast_in_dim.113.clone.1
  821.7 0.7 slice_dynamic-update-slice_fusion
  822.4 1.6 add_dynamic-update-slice_fusion.1
  824.0 22.6 %while.33 = (s32[]{:T(128)}, bf16[64,640]{1,0:T(8,128)(2,1)S(1)}, f32[256,128]{1,0:T(8,128)S(1)}, f32[256,128]{1,0:T(8,128)S(1)}, s32[5]{0:T(128)S(1)}, /*index=...) while((s32[]{:T(128)}, bf16[64,640]{1,0:T(8,128)(2,1)S(1)}, ...), condition=%wide.region_17.18_spmd.clone, body=%wide.region_14.17_spmd.clone.sunk | while | flops 21463112 | bytes 1168988 | solution.py:114
  846.6 1.6 add_dynamic-update-slice_fusion
  848.3 1.5 broadcast_in_dim.113.clone
  849.8 0.7 slice_dynamic-update-slice_fusion.1
  850.4 1.6 add_dynamic-update-slice_fusion.3
  852.0 1.6 add_dynamic-update-slice_fusion.2
  853.6 0.6 slice.34
  854.2 12.0 all-to-all-start.9
  866.3 12.0 all-to-all-done.9
  878.3 15.4 all_to_all.295
  893.7 15.6 all_to_all.296
  909.3 6.4 all-to-all-start.7
  915.7 0.6 copy_bitcast_fusion.3
  916.4 265.4 %reduce-scatter.5.cloned.1.call-done = f32[64,128]{1,0:T(8,128)} async-done(((f32[4096,128]{1,0:T(8,128)}), f32[64,128]{1,0:T(8,128)}) %reduce-scatter.5.cloned.1.call-update) | async-done | bytes 32784 | tf_op jit(solution)/shard_map/reduce_scatter | solution.py:222
  1181.8 1.4 convert_bitcast_fusion
  1183.2 57.3 %all-to-all-start.15 = ((bf16[8,8,128]{2,1,0:T(8,128)(2,1)}), bf16[8,8,128]{2,1,0:T(8,128)(2,1)S(1)}, u32[]{:S(2)}, u32[]{:S(2)}) async-start(bf16[8,8,128]{2,1,0:T(8,128)(2,1)} %convert_bitcast_fusion), calls=%async_computation.17 | async-start | bytes 32768 | tf_op jit(solution)/shard_map/all_to_all | solution.py:244
  1240.5 317.6 %reduce-scatter.3.cloned.1.call-done = f32[64,128]{1,0:T(8,128)} async-done(((f32[4096,128]{1,0:T(8,128)}), f32[64,128]{1,0:T(8,128)}) %reduce-scatter.3.cloned.1.call-update) | async-done | bytes 32784 | tf_op jit(solution)/shard_map/reduce_scatter | solution.py:221
  1558.1 1.4 convert_bitcast_fusion.1
  1559.5 61.2 %all-to-all-start.14 = ((bf16[8,8,128]{2,1,0:T(8,128)(2,1)}), bf16[8,8,128]{2,1,0:T(8,128)(2,1)S(1)}, u32[]{:S(2)}, u32[]{:S(2)}) async-start(bf16[8,8,128]{2,1,0:T(8,128)(2,1)} %convert_bitcast_fusion.1), calls=%async_computation.15 | async-start | bytes 32768 | tf_op jit(solution)/shard_map/all_to_all | solution.py:241
  1620.7 0.6 copy_bitcast_fusion.4
  1621.3 0.8 copy.68
  1622.1 10.5 all-to-all-done.14
  1632.6 0.6 copy.127
  1633.2 0.6 copy.128
  (142 shorter events, 25.0 us)
Async XLA Ops:
  7.2 32.8 %copy-start = (bf16[32,1024]{1,0:T(8,128)(2,1)S(1)}, bf16[32,1024]{1,0:T(8,128)(2,1)}, u32[]{:S(2)}) copy-start(bf16[32,1024]{1,0:T(8,128)(2,1)} %param.19) | copy-start | bytes 196612
  7.2 118.8 %copy-start.1 = (bf16[32,5120]{1,0:T(8,128)(2,1)S(1)}, bf16[32,5120]{1,0:T(8,128)(2,1)}, u32[]{:S(2)}) copy-start(bf16[32,5120]{1,0:T(8,128)(2,1)} %param.21) | copy-start | bytes 983044
  7.2 119.5 %copy-start.7 = (s32[256]{0:T(256)S(1)}, s32[256]{0:T(256)}, u32[]{:S(2)}) copy-start(s32[256]{0:T(256)} %param.28) | copy-start | bytes 3076
  7.2 119.5 %copy-start.6 = (s32[256]{0:T(256)S(1)}, s32[256]{0:T(256)}, u32[]{:S(2)}) copy-start(s32[256]{0:T(256)} %param.31) | copy-start | bytes 3076
  7.2 119.5 %copy-start.5 = (s32[256]{0:T(256)S(1)}, s32[256]{0:T(256)}, u32[]{:S(2)}) copy-start(s32[256]{0:T(256)} %param.29) | copy-start | bytes 3076
  7.2 119.5 %copy-start.8 = (s32[256]{0:T(256)S(1)}, s32[256]{0:T(256)}, u32[]{:S(2)}) copy-start(s32[256]{0:T(256)} %param.30) | copy-start | bytes 3076
  7.2 146.7 %copy-start.2 = (bf16[32,5120]{1,0:T(8,128)(2,1)S(1)}, bf16[32,5120]{1,0:T(8,128)(2,1)}, u32[]{:S(2)}) copy-start(bf16[32,5120]{1,0:T(8,128)(2,1)} %param.18) | copy-start | bytes 983044
  36.0 15.9 all-to-all-start.4
  51.9 102.8 %copy-start.3 = (bf16[8,8,128]{2,0,1:T(8,128)(2,1)}, bf16[8,8,128]{2,0,1:T(8,128)(2,1)S(1)}, u32[]{:S(2)}) copy-start(bf16[8,8,128]{2,0,1:T(8,128)(2,1)S(1)} %all-to-all-done.4) | copy-start | bytes 49156
  51.9 16.4 all-to-all-start.2
  55.8 317.5 %all-gather.3.cloned.1.call-start = ((), (), s32[]{:S(2)}) async-start(), calls=%async_computation.18 | async-start | bytes 1064960 | tf_op jit(solution)/shard_map/all_gather | solution.py:167
  102.9 18.3 %all-to-all-start.12 = ((bf16[8,8,640]{2,0,1:T(8,128)(2,1)}), bf16[8,8,640]{2,0,1:T(8,128)(2,1)S(1)}, u32[]{:S(2)}, u32[]{:S(2)}) async-start(bf16[8,8,640]{2,0,1:T(8,128)(2,1)} %bitcast.152), calls=%async_computation.12 | async-start | bytes 163840 | tf_op jit(solution)/shard_map/all_to_all | solution.py:156
  121.1 20.9 %all-to-all-start.3 = ((bf16[32,8,640]{2,0,1:T(8,128)(2,1)}), bf16[32,8,640]{2,0,1:T(8,128)(2,1)S(1)}, u32[]{:S(2)}, u32[]{:S(2)}) async-start(bf16[32,8,640]{2,0,1:T(8,128)(2,1)} %bitcast.104), calls=%async_computation.3 | async-start | bytes 655360 | tf_op jit(solution)/shard_map/all_to_all | solution.py:152
  142.1 26.2 %all-to-all-start.6 = ((bf16[32,8,640]{2,0,1:T(8,128)(2,1)}), bf16[32,8,640]{2,0,1:T(8,128)(2,1)S(1)}, u32[]{:S(2)}, u32[]{:S(2)}) async-start(bf16[32,8,640]{2,0,1:T(8,128)(2,1)} %bitcast.103), calls=%async_computation.6 | async-start | bytes 655360 | tf_op jit(solution)/shard_map/all_to_all | solution.py:151
  151.3 581.2 %all-gather.5.cloned.1.call-start = ((), (), s32[]{:S(2)}) async-start(), calls=%async_computation.19 | async-start | bytes 1064960 | tf_op jit(solution)/shard_map/all_gather | solution.py:168
  168.3 565.7 %all-to-all-start = ((bf16[32,8,640]{2,0,1:T(8,128)(2,1)}), bf16[32,8,640]{2,0,1:T(8,128)(2,1)S(1)}, u32[]{:S(2)}, u32[]{:S(2)}) async-start(bf16[32,8,640]{2,0,1:T(8,128)(2,1)} %bitcast.105), calls=%async_computation | async-start | bytes 655360 | tf_op jit(solution)/shard_map/all_to_all | solution.py:148
  734.0 90.0 %all-to-all-start.10 = ((bf16[8,8,640]{2,0,1:T(8,128)(2,1)}), bf16[8,8,640]{2,0,1:T(8,128)(2,1)S(1)}, u32[]{:S(2)}, u32[]{:S(2)}) async-start(bf16[8,8,640]{2,0,1:T(8,128)(2,1)} %bitcast.153), calls=%async_computation.10 | async-start | bytes 163840 | tf_op jit(solution)/shard_map/all_to_all | solution.py:153
  788.9 392.8 %reduce-scatter.5.cloned.1.call-start = ((), (), s32[]{:S(2)}) async-start(), calls=%async_computation.21 | async-start | bytes 2129920 | tf_op jit(solution)/shard_map/reduce_scatter | solution.py:222
  820.3 3.7 copy-start.4
  848.2 709.9 %reduce-scatter.3.cloned.1.call-start = ((), (), s32[]{:S(2)}) async-start(), calls=%async_computation.20 | async-start | bytes 2129920 | tf_op jit(solution)/shard_map/reduce_scatter | solution.py:221
  854.2 24.1 %all-to-all-start.9 = ((bf16[8,32,128]{2,1,0:T(8,128)(2,1)}), bf16[8,32,128]{2,1,0:T(8,128)(2,1)S(1)}, u32[]{:S(2)}, u32[]{:S(2)}) async-start(bf16[8,32,128]{2,1,0:T(8,128)(2,1)} %bitcast.20), calls=%async_computation.9 | async-start | bytes 131072 | tf_op jit(solution)/shard_map/all_to_all | solution.py:233
  909.3 273.8 %all-to-all-start.7 = ((bf16[8,32,640]{2,1,0:T(8,128)(2,1)}), bf16[8,32,640]{2,1,0:T(8,128)(2,1)S(1)}, u32[]{:S(2)}, u32[]{:S(2)}) async-start(bf16[8,32,640]{2,1,0:T(8,128)(2,1)} %bitcast.16), calls=%async_computation.7 | async-start | bytes 655360 | tf_op jit(solution)/shard_map/all_to_all | solution.py:225
  1183.2 376.3 %all-to-all-start.15 = ((bf16[8,8,128]{2,1,0:T(8,128)(2,1)}), bf16[8,8,128]{2,1,0:T(8,128)(2,1)S(1)}, u32[]{:S(2)}, u32[]{:S(2)}) async-start(bf16[8,8,128]{2,1,0:T(8,128)(2,1)} %convert_bitcast_fusion), calls=%async_computation.17 | async-start | bytes 32768 | tf_op jit(solution)/shard_map/all_to_all | solution.py:244
  1559.5 73.1 %all-to-all-start.14 = ((bf16[8,8,128]{2,1,0:T(8,128)(2,1)}), bf16[8,8,128]{2,1,0:T(8,128)(2,1)S(1)}, u32[]{:S(2)}, u32[]{:S(2)}) async-start(bf16[8,8,128]{2,1,0:T(8,128)(2,1)} %convert_bitcast_fusion.1), calls=%async_computation.15 | async-start | bytes 32768 | tf_op jit(solution)/shard_map/all_to_all | solution.py:241
Sparse Core Ops, SparseCore 0:
  58.7 314.5 all-gather.2
  376.0 356.3 all-gather.4
  848.4 333.3 reduce-scatter.4
  1184.7 373.3 reduce-scatter.2
where the time goes:
time: 1640 us
  waiting for transfers between devices  1220 us (74%)
  starting transfers between devices  230 us (14%)
  blocking collectives  94.4 us (6%)
  loops' own time  26.5 us (2%)
  local copies, waits for them, and re-layouts  24.2 us (1%)
  matrix products  17.8 us (1%)
  between operations  16.6 us (1%)
  other arithmetic  16.5 us (1%)
    all_gather x1, waiting for transfers between devices, local(): lax.all_gather(lead_v, 'dp', axis=0, tiled=True)  358 us
    reduce_scatter x1, waiting for transfers between devices, local(): lax.psum_scatter(partial_key, 'dp', scatter_dimension=0, tiled=True)  318 us
    reduce_scatter x1, waiting for transfers between devices, local(): lax.psum_scatter(partial_value, 'dp', scatter_dimension=0, tiled=True)  265 us
    all_gather x1, waiting for transfers between devices, local(): lax.all_gather(lead_k, 'dp', axis=0, tiled=True)  191 us
    all_to_all x1, starting transfers between devices, local(): lax.all_to_all(summed_key.astype(jnp.bfloat16), 'head', split_axis=0, con...  61.2 us
    all_to_all x1, starting transfers between devices, local(): lax.all_to_all(summed_value.astype(jnp.bfloat16), 'head', split_axis=0, c...  57.3 us
    all_to_all x1, starting transfers between devices, local(): lax.all_to_all(prompt_q, 'head', split_axis=1, concat_axis=0, tiled=True)  54.9 us
  transfers between devices with their start and end apart: 15, of which 11 were waited for; matrix products, arithmetic and copies ran while one was open for 3% of the time, Pallas kernels for 0%

commit v1 on v0

v1 whole, which is shorter than its diff:
```python
import jax
import jax.numpy as jnp
from jax import lax
from jax.experimental import pallas as pl
from jax.experimental.pallas import tpu as pltpu
from jax.sharding import PartitionSpec as P

D = 128
QPK = 5
W = QPK * D
PROMPT = 256
MASKED = -1e30
SCALE = D**-0.5
MESH = pl.DeviceIdType.MESH
BF = jnp.bfloat16
F32 = jnp.float32


def coords():
    dp = lax.axis_index("dp")
    hd = lax.axis_index("head")
    x, zl, y = lax.rem(dp, 4), lax.rem(dp // 4, 4), dp // 16
    zh, c = hd // 2, lax.rem(hd, 2)
    return x, y, zh * 4 + zl, c


def place(x, y, z, c):
    return ((y * 4 + lax.rem(z, 4)) * 4 + x, (z // 4) * 2 + c)


def wrap(a, n):
    return lax.rem(a + 4 * n, n)


def remote(src, dst, send_sem, recv_sem, device):
    return pltpu.make_async_remote_copy(
        src_ref=src,
        dst_ref=dst,
        send_sem=send_sem,
        recv_sem=recv_sem,
        device_id=device,
        device_id_type=MESH,
    )


class Peers:
    def __init__(self):
        self.x, self.y, self.z, self.c = coords()
        self.s = 2 * self.x + self.c
        x, y, z, c, s = self.x, self.y, self.z, self.c, self.s
        self.group = [wrap(s + d, 8) for d in range(1, 8)]
        self.group_dev = [place(g // 2, y, z, lax.rem(g, 2)) for g in self.group]
        self.sender = [wrap(s - d, 8) for d in range(1, 8)]
        self.y_dev = [place(x, wrap(y + d, 4), z, c) for d in range(1, 4)]
        self.up = place(x, y, wrap(z + 1, 16), c)
        self.down = place(x, y, wrap(z - 1, 16), c)
        self.up4 = place(x, y, wrap(z + 4, 16), c)
        self.down4 = place(x, y, wrap(z - 4, 16), c)

    def signal_all(self):
        barrier = pltpu.get_barrier_semaphore()
        peers = [*self.group_dev, *self.y_dev, self.up, self.down, self.up4, self.down4]
        for peer in peers:
            pl.semaphore_signal(barrier, inc=1, device_id=peer, device_id_type=MESH)
        return barrier, len(peers)


def head_sums(o_ref, do_ref, rows):
    lane = lax.broadcasted_iota(jnp.int32, (rows, D), 1)
    total = jnp.zeros((rows, D), F32)
    for g in range(8 * QPK):
        cols = slice(g * D, (g + 1) * D)
        one = jnp.sum(o_ref[:, cols].astype(F32) * do_ref[:, cols].astype(F32), axis=1, keepdims=True)
        total = jnp.where(lane == g, one, total)
    return total


def gather_kernel(
    rq, rk, rv, ro, rdo, pq, pk, pv, po, pdo,
    rq_o, rdo_o, rkv_o, prev_o, g_o, pqd_o, dl_o,
    pkv_s, pqd_s, dl_s,
    a_send, a_recv, own_sem, sh_send, sh_recv, r_send, r_recv, l_send, l_recv, y_send, y_recv,
):
    me = Peers()
    s, y, z = me.s, me.y, me.z
    barrier, count = me.signal_all()
    for g in range(8):
        k8 = pk[:, g * D : (g + 1) * D].astype(F32)
        v8 = pv[:, g * D : (g + 1) * D].astype(F32)
        pkv_s[g] = jnp.concatenate([k8, v8], axis=0).astype(BF)
    for g in range(8):
        parts = [pq[:, (g * QPK + i) * D : (g * QPK + i + 1) * D].astype(F32) for i in range(QPK)]
        parts += [pdo[:, (g * QPK + i) * D : (g * QPK + i + 1) * D].astype(F32) for i in range(QPK)]
        pqd_s[g] = jnp.concatenate(parts, axis=0).astype(BF)
    sums = jnp.concatenate(
        [head_sums(ro, rdo, 32), head_sums(po, pdo, 8), jnp.zeros((D - 40, D), F32)], axis=0
    ).T
    for g in range(8):
        dl_s[g, 0:QPK, :] = sums[g * QPK : (g + 1) * QPK, :]
        dl_s[g, QPK:8, :] = jnp.zeros((8 - QPK, D), F32)
    pl.semaphore_wait(barrier, count)

    def cols(ref, h, width):
        return ref.at[:, pl.ds(pl.multiple_of(h * width, D), width)]

    mine = (y * 4 + lax.rem(z, 4), z // 4)
    sources = [
        lambda h: pkv_s.at[h],
        lambda h: cols(rk, h, D),
        lambda h: cols(rv, h, D),
        lambda h: cols(rq, h, W),
        lambda h: cols(rdo, h, W),
        lambda h: pqd_s.at[h],
        lambda h: dl_s.at[h],
    ]
    landing = [
        lambda j: g_o.at[mine[0], mine[1], j],
        lambda j: rkv_o.at[0, j],
        lambda j: rkv_o.at[1, j],
        lambda j: rq_o.at[j],
        lambda j: rdo_o.at[j],
        lambda j: pqd_o.at[j],
        lambda j: dl_o.at[j],
    ]
    kinds = range(len(sources))
    own = [pltpu.make_async_copy(sources[n](s), landing[n](s), own_sem.at[n]) for n in kinds]
    sent = []
    for n in kinds:
        own[n].start()
        for d in range(7):
            h = me.group[d]
            copy = remote(sources[n](h), landing[n](s), a_send.at[n, d], a_recv.at[n, s], me.group_dev[d])
            copy.start()
            sent.append(copy)

    def arrived(n):
        own[n].wait()
        for d in range(7):
            j = me.sender[d]
            remote(landing[n](j), landing[n](j), a_send.at[n, d], a_recv.at[n, j], me.group_dev[d]).wait_recv()

    def block(yy, zz):
        return g_o.at[yy * 4 + lax.rem(zz, 4), zz // 4]

    def spread(zz):
        for d in range(3):
            copy = remote(block(y, zz), block(y, zz), y_send.at[zz, d], y_recv.at[zz, d], me.y_dev[d])
            copy.start()
            sent.append(copy)

    arrived(0)
    for t in range(9):
        zr, zl = wrap(z - t, 16), wrap(z + t, 16)
        if t > 0:
            remote(block(y, zr), block(y, zr), r_send.at[t - 1], r_recv.at[t - 1], me.up).wait_recv()
        if t < 8:
            copy = remote(block(y, zr), block(y, zr), r_send.at[t], r_recv.at[t], me.up)
            copy.start()
            sent.append(copy)
        if 0 < t < 8:
            remote(block(y, zl), block(y, zl), l_send.at[t - 1], l_recv.at[t - 1], me.down).wait_recv()
        if t < 7:
            copy = remote(block(y, zl), block(y, zl), l_send.at[t], l_recv.at[t], me.down)
            copy.start()
            sent.append(copy)
        spread(zr)
        if 0 < t < 8:
            spread(zl)
        if t == 1:
            arrived(1)
            arrived(2)
            shift = remote(rkv_o, prev_o, sh_send, sh_recv, me.up4)
            shift.start()
    for n in range(3, len(sources)):
        arrived(n)
    shift.wait()
    for zz in range(16):
        for d in range(3):
            there = block(wrap(y - d - 1, 4), zz)
            remote(there, there, y_send.at[zz, d], y_recv.at[zz, d], me.y_dev[d]).wait_recv()
    for copy in sent:
        copy.wait_send()


def dot_t(a, b):
    return lax.dot_general(a, b, (((1,), (1,)), ((), ())), preferred_element_type=F32)


def dot(a, b):
    return lax.dot_general(a, b, (((1,), (0,)), ((), ())), preferred_element_type=F32)


def t_dot(a, b):
    return lax.dot_general(a, b, (((0,), (0,)), ((), ())), preferred_element_type=F32)


def grads(q, do, delta, k, v, bias, filled):
    scores = dot_t(q, k) * SCALE + bias
    highest = jnp.max(scores, axis=1, keepdims=True)
    e = jnp.exp(scores - highest)
    total = jnp.sum(e, axis=1, keepdims=True)
    likely = e * jnp.where(filled, 1.0 / total, 0.0)
    prob_grad = dot_t(do, v)
    score_grad = (likely * (prob_grad - delta)).astype(BF)
    dq = dot(score_grad, k) * SCALE
    dk = t_dot(score_grad, q) * SCALE
    dv = t_dot(likely.astype(BF), do)
    return dq, dk, dv


def compute_kernel(
    tab, rq, rdo, rkv, prev, g, pqd, dl,
    dq_o, cur_o, prev_d, dense_o, pdq_o,
    acc,
):
    x, y, z, c = coords()
    zl, zh = lax.rem(z, 4), z // 4
    acc[...] = jnp.zeros_like(acc)
    tab_row = tab[...].astype(F32)
    tab_col = tab_row.T

    def stack(parts):
        return jnp.concatenate(parts, axis=0)

    def prompt_rows(p):
        kv = g[p].astype(F32)
        return kv[:, 0:8, :].reshape(PROMPT, D).astype(BF), kv[:, 8:16, :].reshape(PROMPT, D).astype(BF)

    def add(p, dk, dv):
        acc[p, :, 0:8, :] += dk.reshape(32, 8, D)
        acc[p, :, 8:16, :] += dv.reshape(32, 8, D)

    def one_rank(r, _):
        rank = ((y * 4 + zl) * 4 + r).astype(F32)
        base = zh * 64
        holding = tab_row[2:3, :] == rank
        owner = tab_row[1:2, :]
        first_f = jnp.min(jnp.where(holding, owner, 16.0))
        last_f = jnp.max(jnp.where(holding, owner, 0.0))
        first, last = first_f.astype(jnp.int32), last_f.astype(jnp.int32)
        row = (lax.broadcasted_iota(jnp.int32, (64, PROMPT), 0) + base).astype(F32)
        label = (lax.broadcasted_iota(jnp.int32, (64, PROMPT), 1) + 1).astype(F32)
        start, stop = tab_row[3:4, :], tab_row[3:4, :] + tab_row[0:1, :]
        member = holding & (row >= start) & (row < stop)
        seg_q = jnp.sum(jnp.where(member, label, 0.0), axis=1, keepdims=True)
        owner_q = jnp.sum(jnp.where(member, jnp.broadcast_to(owner, member.shape), 0.0), axis=1, keepdims=True)
        key_row = (lax.broadcasted_iota(jnp.int32, (PROMPT, D), 1) + base - 64).astype(F32)
        key_label = (lax.broadcasted_iota(jnp.int32, (PROMPT, D), 0) + 1).astype(F32)
        start_c, stop_c = tab_col[:, 3:4], tab_col[:, 3:4] + tab_col[:, 0:1]
        key_member = (tab_col[:, 2:3] == rank) & (key_row >= start_c) & (key_row < stop_c)
        seg_k = jnp.sum(jnp.where(key_member, key_label, 0.0), axis=0, keepdims=True)
        filled = seg_q > 0.0
        q_pos = lax.broadcasted_iota(jnp.int32, (64, D), 0) + 64
        k_pos = lax.broadcasted_iota(jnp.int32, (64, D), 1)
        own = (seg_q == seg_k) & filled & (k_pos <= q_pos)
        take_first = filled & (owner_q == first_f)
        take_last = filled & (owner_q == last_f) & (first_f != last_f)
        bias = jnp.concatenate(
            [
                jnp.broadcast_to(jnp.where(take_first, 0.0, MASKED), (64, PROMPT)),
                jnp.broadcast_to(jnp.where(take_last, 0.0, MASKED), (64, PROMPT)),
                jnp.where(own, 0.0, MASKED),
            ],
            axis=1,
        )
        bias = stack([bias] * QPK)
        filled5 = stack([jnp.where(filled, 1.0, 0.0)] * QPK) > 0.0
        two = pl.ds(2 * r, 2)
        q2 = rq[two].reshape(64, W)
        do2 = rdo[two].reshape(64, W)
        q = stack([q2[:, i * D : (i + 1) * D] for i in range(QPK)])
        do = stack([do2[:, i * D : (i + 1) * D] for i in range(QPK)])
        dl2 = dl[two]
        dl0, dl1 = dl2[0].T, dl2[1].T
        delta = stack([part[0:32, i : i + 1] for i in range(QPK) for part in (dl0, dl1)])
        k1, v1 = prompt_rows(first)
        k2, v2 = prompt_rows(last)
        k = stack([k1, k2, prev[0, two].reshape(64, D), rkv[0, two].reshape(64, D)])
        v = stack([v1, v2, prev[1, two].reshape(64, D), rkv[1, two].reshape(64, D)])
        dq, dk, dv = grads(q, do, delta, k, v, bias, filled5)
        dq = dq.astype(BF)
        dq_o[two] = jnp.concatenate([dq[i * 64 : (i + 1) * 64] for i in range(QPK)], axis=1).reshape(2, 32, W)
        add(first, dk[0:256], dv[0:256])
        add(last, dk[256:512], dv[256:512])
        prev_d[0, two] = dk[512:576].astype(BF).reshape(2, 32, D)
        prev_d[1, two] = dv[512:576].astype(BF).reshape(2, 32, D)
        cur_o[0, two] = dk[576:640].reshape(2, 32, D)
        cur_o[1, two] = dv[576:640].reshape(2, 32, D)
        return 0

    lax.fori_loop(0, 4, one_rank, 0)

    p = y * 4 + zl
    lead = pqd[...].astype(F32)
    q = stack([lead[:, i * 8 : i * 8 + 8, :].reshape(64, D) for i in range(QPK)]).astype(BF)
    do = stack([lead[:, (i + 5) * 8 : (i + 5) * 8 + 8, :].reshape(64, D) for i in range(QPK)]).astype(BF)
    dls = [dl[j].T for j in range(8)]
    delta = stack([dls[j][32:40, i : i + 1] for i in range(QPK) for j in range(8)])

    def place_of(n, hi):
        j, i = (n // 8) % 8, n % 8
        return (j // 2) * 64 + (hi * 2 + j % 2) * 8 + i

    n_q = lax.broadcasted_iota(jnp.int32, (64, PROMPT), 0)
    n_k = lax.broadcasted_iota(jnp.int32, (64, PROMPT), 1)
    bias = jnp.where(place_of(n_k, n_k // 64) <= place_of(n_q, zh), 0.0, MASKED)
    k, v = prompt_rows(p)
    dq, dk, dv = grads(q, do, delta, k, v, stack([bias] * QPK), True)
    add(p, dk, dv)
    for j in range(8):
        tiles = [dq[i * 64 + j * 8 : i * 64 + j * 8 + 8] for i in range(QPK)]
        pdq_o[j] = stack([*tiles, jnp.zeros((8, D), F32)]).astype(BF)
    dense_o[...] = acc[...].astype(BF)


def scatter_kernel(
    dq, cur, prev_d, dense, pdq,
    dq_o, dk_o, dv_o, pdq_o, pdk_o, pdv_o,
    back, y_in, r_out, r_in, l_out, l_in, kv_s, pkv_s, pdq_in, pkv_in,
    a_send, a_recv, own_sem, sh_send, sh_recv, r_send, r_recv, l_send, l_recv, y_send, y_recv,
):
    me = Peers()
    s, y, z = me.s, me.y, me.z
    barrier, count = me.signal_all()
    pl.semaphore_wait(barrier, count)
    sent = []

    def cols(ref, h, width):
        return ref.at[:, pl.ds(pl.multiple_of(h * width, D), width)]

    def block(yy, zz):
        return (yy * 4 + lax.rem(zz, 4), zz // 4)

    order = []
    for t in range(8):
        order.append(8 - t)
        if t < 7:
            order.append(-7 + t)
    order.append(0)
    targets = {k: wrap(z + k, 16) for k in order}

    def exchange(k):
        zz = targets[k]
        for d in range(3):
            there = block(wrap(y + d + 1, 4), zz)
            copy = remote(dense.at[there[0], there[1]], y_in.at[d, zz], y_send.at[zz, d], y_recv.at[zz, d], me.y_dev[d])
            copy.start()
            sent.append(copy)

    for k in order[:4]:
        exchange(k)
    shift = remote(prev_d, back, sh_send, sh_recv, me.down4)
    shift.start()
    for k in order[4:]:
        exchange(k)

    sources = [
        lambda h: dq.at[h],
        lambda h: pdq.at[h],
        lambda h: kv_s.at[0, h],
        lambda h: kv_s.at[1, h],
        lambda h: pkv_s.at[h],
    ]
    landing = [
        lambda j: cols(dq_o, j, W),
        lambda j: pdq_in.at[j],
        lambda j: cols(dk_o, j, D),
        lambda j: cols(dv_o, j, D),
        lambda j: pkv_in.at[j],
    ]
    own = {}

    def send(n):
        own[n] = pltpu.make_async_copy(sources[n](s), landing[n](s), own_sem.at[n])
        own[n].start()
        for d in range(7):
            h = me.group[d]
            copy = remote(sources[n](h), landing[n](s), a_send.at[n, d], a_recv.at[n, s], me.group_dev[d])
            copy.start()
            sent.append(copy)

    def arrived(n):
        own[n].wait()
        for d in range(7):
            j = me.sender[d]
            remote(landing[n](j), landing[n](j), a_send.at[n, d], a_recv.at[n, j], me.group_dev[d]).wait_recv()

    send(0)
    send(1)

    def partial(k):
        zz = targets[k]
        here = block(y, zz)
        total = dense[here[0], here[1]].astype(F32)
        for d in range(3):
            remote(y_in.at[d, zz], y_in.at[d, zz], y_send.at[zz, d], y_recv.at[zz, d], me.y_dev[d]).wait_recv()
            total += y_in[d, zz].astype(F32)
        return total

    def r_arrival(t):
        remote(r_in.at[t], r_in.at[t], r_send.at[t], r_recv.at[t], me.up).wait_recv()
        return r_in[t].astype(F32)

    def l_arrival(t):
        remote(l_in.at[t], l_in.at[t], l_send.at[t], l_recv.at[t], me.down).wait_recv()
        return l_in[t].astype(F32)

    for t in range(8):
        total = partial(8 - t)
        if t > 0:
            total += r_arrival(t - 1)
        r_out[t] = total.astype(BF)
        copy = remote(r_out.at[t], r_in.at[t], r_send.at[t], r_recv.at[t], me.up)
        copy.start()
        sent.append(copy)
        if t < 7:
            total = partial(-7 + t)
            if t > 0:
                total += l_arrival(t - 1)
            l_out[t] = total.astype(BF)
            copy = remote(l_out.at[t], l_in.at[t], l_send.at[t], l_recv.at[t], me.down)
            copy.start()
            sent.append(copy)
        if t == 4:
            shift.wait_recv()
            kv_s[...] = (cur[...] + back[...].astype(F32)).astype(BF)
            send(2)
            send(3)
    total = partial(0) + r_arrival(7) + l_arrival(6)
    pkv_s[...] = total.astype(BF)
    send(4)
    arrived(1)
    for h in range(8):
        tiles = pdq_in[h].astype(F32)
        for i in range(QPK):
            pdq_o[:, (h * QPK + i) * D : (h * QPK + i + 1) * D] = tiles[i * 8 : i * 8 + 8].astype(BF)
    arrived(0)
    arrived(2)
    arrived(3)
    arrived(4)
    for h in range(8):
        tile = pkv_in[h].astype(F32)
        pdk_o[:, h * D : (h + 1) * D] = tile[0:8].astype(BF)
        pdv_o[:, h * D : (h + 1) * D] = tile[8:16].astype(BF)
    shift.wait_send()
    for copy in sent:
        copy.wait_send()


def vmem(n):
    return [pl.BlockSpec(memory_space=pltpu.VMEM)] * n


def shapes(*items):
    return [jax.ShapeDtypeStruct(shape, dtype) for shape, dtype in items]


def local(
    response_q, response_k, response_v, response_o, response_do,
    prompt_q, prompt_k, prompt_v, prompt_o, prompt_do,
    resp_len, resp_prompt, plan_rank, plan_offset,
):
    dma = pltpu.SemaphoreType.DMA
    limit = 40 * 2**20
    rq, rdo, rkv, prev, g, pqd, dl = pl.pallas_call(
        gather_kernel,
        out_shape=shapes(
            ((8, 32, W), BF),
            ((8, 32, W), BF),
            ((2, 8, 32, D), BF),
            ((2, 8, 32, D), BF),
            ((16, 4, 8, 16, D), BF),
            ((8, 80, D), BF),
            ((8, 8, D), F32),
        ),
        in_specs=vmem(10),
        out_specs=vmem(7),
        scratch_shapes=[
            pltpu.VMEM((8, 16, D), BF),
            pltpu.VMEM((8, 80, D), BF),
            pltpu.VMEM((8, 8, D), F32),
            dma((7, 7)),
            dma((7, 8)),
            dma((7,)),
            dma,
            dma,
            dma((8,)),
            dma((8,)),
            dma((7,)),
            dma((7,)),
            dma((16, 3)),
            dma((16, 3)),
        ],
        compiler_params=pltpu.CompilerParams(collective_id=0, has_side_effects=True, vmem_limit_bytes=limit),
        name="exchange_in",
    )(
        response_q, response_k, response_v, response_o, response_do,
        prompt_q, prompt_k, prompt_v, prompt_o, prompt_do,
    )
    zero = jnp.zeros_like(resp_len)
    tab = jnp.stack([resp_len, resp_prompt, plan_rank, plan_offset, zero, zero, zero, zero])
    dq, cur, prev_d, dense, pdq = pl.pallas_call(
        compute_kernel,
        out_shape=shapes(
            ((8, 32, W), BF),
            ((2, 8, 32, D), F32),
            ((2, 8, 32, D), BF),
            ((16, 32, 16, D), BF),
            ((8, 48, D), BF),
        ),
        in_specs=vmem(8),
        out_specs=vmem(5),
        scratch_shapes=[pltpu.VMEM((16, 32, 16, D), F32)],
        compiler_params=pltpu.CompilerParams(vmem_limit_bytes=limit),
        name="attention_grads",
    )(tab, rq, rdo, rkv, prev, g.reshape(16, 32, 16, D), pqd, dl)
    return tuple(
        pl.pallas_call(
            scatter_kernel,
            out_shape=shapes(
                ((32, 40 * D), BF),
                ((32, 8 * D), BF),
                ((32, 8 * D), BF),
                ((8, 40 * D), BF),
                ((8, 8 * D), BF),
                ((8, 8 * D), BF),
            ),
            in_specs=vmem(5),
            out_specs=vmem(6),
            scratch_shapes=[
                pltpu.VMEM((2, 8, 32, D), BF),
                pltpu.VMEM((3, 16, 8, 16, D), BF),
                pltpu.VMEM((8, 8, 16, D), BF),
                pltpu.VMEM((8, 8, 16, D), BF),
                pltpu.VMEM((7, 8, 16, D), BF),
                pltpu.VMEM((7, 8, 16, D), BF),
                pltpu.VMEM((2, 8, 32, D), BF),
                pltpu.VMEM((8, 16, D), BF),
                pltpu.VMEM((8, 48, D), BF),
                pltpu.VMEM((8, 16, D), BF),
                dma((5, 7)),
                dma((5, 8)),
                dma((5,)),
                dma,
                dma,
                dma((8,)),
                dma((8,)),
                dma((7,)),
                dma((7,)),
                dma((16, 3)),
                dma((16, 3)),
            ],
            compiler_params=pltpu.CompilerParams(collective_id=1, has_side_effects=True, vmem_limit_bytes=limit),
            name="exchange_out",
        )(dq, cur, prev_d, dense.reshape(16, 4, 8, 16, D), pdq)
    )


def solution(mesh):
    rows = P(("dp", "head"), None)
    return jax.shard_map(
        local,
        mesh=mesh,
        in_specs=(rows,) * 10 + (P(),) * 4,
        out_specs=(rows,) * 6,
        check_vma=False,
    )
```

time: 1640 us -> 122 us (0.07)
  waiting for transfers between devices: 1220 us -> 0 us
  starting transfers between devices: 230 us -> 0 us
  Pallas kernels: 0 us -> 107 us
  blocking collectives: 94.4 us -> 0 us
  loops' own time: 26.5 us -> 0 us
  matrix products: 17.8 us -> 0 us
  other arithmetic: 16.5 us -> 0 us
    reduce_scatter x2 -> x0, waiting for transfers between devices: 583 us -> none  [the longest x1 318 us: local(): lax.psum_scatter(partial_key, 'dp', scatter_dimension=0, tiled=True)]
    all_gather x2 -> x0, waiting for transfers between devices: 549 us -> none  [the longest x1 358 us: local(): lax.all_gather(lead_v, 'dp', axis=0, tiled=True)]
    all_to_all x11 -> x0, starting transfers between devices: 230 us -> none  [the longest x1 61.2 us: local(): lax.all_to_all(summed_key.astype(jnp.bfloat16), 'head', split_axis=0, con...]
    pallas_call x0 -> x3, Pallas kernels: none -> 107 us  [the longest x1 53.8 us: local(): pl.pallas_call(gather_kernel, out_shape=shapes(((8, 32, W), BF), ((8, 32,...]
    all_to_all x5 -> x0, blocking collectives: 94.4 us -> none  [the longest x1 28.7 us: local(): lax.all_to_all(prompt_k, 'head', split_axis=1, concat_axis=0, tiled=True)]
    all_to_all x11 -> x0, waiting for transfers between devices: 82.2 us -> none  [the longest x1 14.5 us: local(): lax.all_to_all(response_do, 'head', split_axis=1, concat_axis=0, tiled=True)]
    another operation x2 -> x0, loops' own time: 26.5 us -> none  [group_grads(): lax.scan(advance, start_state, jnp.arange(QUERY_PER_KV, dtype=jnp.int32))]
    dot_general x50 -> x0, matrix products: 17.8 us -> none  [the longest x10 5.18 us: head_grads(): jnp.einsum('qk,kd->qd', score_grad, key_row_block, preferred_element_type...]
  transfers between devices with their start and end apart: 15 -> 0, of which waited for: 11 -> 0; matrix products, arithmetic and copies ran while one was open for 3% -> 0% of each run, Pallas kernels for 0% -> 0%
where the time goes in v1:
time: 122 us; the launch traced here: 121 us
  Pallas kernels  107 us (88%)
  local copies, waits for them, and re-layouts  13.3 us (11%)
    pallas_call x1, Pallas kernels, local(): pl.pallas_call(gather_kernel, out_shape=shapes(((8, 32, W), BF), ((8, 32,...  53.8 us
    pallas_call x1, Pallas kernels, local(): pl.pallas_call(scatter_kernel, out_shape=shapes(((32, 40 * D), BF), ((32,...  46.7 us
    unnamed x26, local copies, waits for them, and re-layouts  12.5 us
    pallas_call x1, Pallas kernels, local(): pl.pallas_call(compute_kernel, out_shape=shapes(((8, 32, W), BF), ((2, 8,...  6.84 us

profile of v1, /device:TPU:1, one launch (start us, length us, event | category | flops | bytes accessed | tf_op | source)
XLA Modules:
  0.0 121.3 jit_solution(1687142860327925171)
XLA Ops:
  0.6 0.7 stack.23.tab
  1.4 0.0 copy-start
  1.4 1.0 copy-done
  2.4 0.0 copy-start.1
  2.4 1.0 copy-done.1
  3.3 0.0 copy-start.2
  3.3 1.0 copy-done.2
  4.3 0.0 copy-start.3
  4.3 0.9 copy-done.3
  5.2 0.0 copy-start.4
  5.2 0.9 copy-done.4
  6.1 0.0 copy-start.5
  6.1 0.9 copy-done.5
  7.0 0.0 copy-start.6
  7.0 0.8 copy-done.6
  7.8 0.0 copy-start.7
  7.8 0.8 copy-done.7
  8.7 0.0 copy-start.8
  8.7 0.7 copy-done.8
  9.4 0.0 copy-start.9
  9.4 0.7 copy-done.9
  10.1 53.8 %exchange_in.1 = (bf16[8,32,640]{2,1,0:T(8,128)(2,1)S(1)}, bf16[8,32,640]{2,1,0:T(8,128)(2,1)S(1)}, bf16[2,8,32,128]{3,2,1,0:T(8,128)(2,1)S(1)}, bf16[2,8,32,128...) custom-call(bf16[32,5120]{1,0:T(8,128)(2,1)S(1)} %copy-done, ...), custom_call_target="tpu_custom_call" | custom-call | tf_op jit(solution)/shard_map/exchange_in/pallas_call | solution.py:465
  63.9 6.8 %attention_grads.1 = (bf16[8,32,640]{2,1,0:T(8,128)(2,1)S(1)}, f32[2,8,32,128]{3,2,1,0:T(8,128)S(1)}, bf16[2,8,32,128]{3,2,1,0:T(8,128)(2,1)S(1)}, bf16[16,32,16...) custom-call(s32[8,256]{1,0:T(8,128)S(1)} %stack.23.tab, bf16[8,32,640]{2,1,0:T(8,128)(2,1)S(1)} %get-tuple-element.18.rq, ...), custom_call_target="tpu_custom_call" | custom-call | tf_op jit(solution)/shard_map/attention_grads/pallas_call | solution.py:502
  70.7 46.7 %exchange_out.1 = (bf16[32,5120]{1,0:T(8,128)(2,1)S(1)}, bf16[32,1024]{1,0:T(8,128)(2,1)S(1)}, bf16[32,1024]{1,0:T(8,128)(2,1)S(1)}, bf16[8,5120]{1,0:T(8,128)(2...) custom-call(bf16[8,32,640]{2,1,0:T(8,128)(2,1)S(1)} %get-tuple-element.25.dq, ...), custom_call_target="tpu_custom_call" | custom-call | tf_op jit(solution)/shard_map/exchange_out/pallas_call | solution.py:518
  117.4 0.7 copy.26
  118.2 0.6 copy.27
  118.8 0.6 copy.28
  119.4 0.6 copy.29
  120.1 0.6 copy.30
  120.7 0.6 copy.31
  (1 shorter events, 0.0 us)
Async XLA Ops:
  1.4 1.0 copy-start
  2.4 1.0 copy-start.1
  3.3 1.0 copy-start.2
  4.3 0.9 copy-start.3
  5.2 0.9 copy-start.4
  6.1 0.9 copy-start.5
  7.0 0.8 copy-start.6
  7.8 0.8 copy-start.7
  8.7 0.7 copy-start.8
  9.4 0.7 copy-start.9

commit v2 on v1

v2 whole, which is shorter than its diff:
```python
import jax
import jax.numpy as jnp
from jax import lax
from jax.experimental import pallas as pl
from jax.experimental.pallas import tpu as pltpu
from jax.sharding import PartitionSpec as P

D = 128
QPK = 5
W = QPK * D
PROMPT = 256
MASKED = -1e30
SCALE = D**-0.5
STEP = (0, 4, -4, 8)
NEAR = (0, 1, 2, -1)
MESH = pl.DeviceIdType.MESH
BF = jnp.bfloat16
F32 = jnp.float32


def coords():
    dp = lax.axis_index("dp")
    hd = lax.axis_index("head")
    x, zl, y = lax.rem(dp, 4), lax.rem(dp // 4, 4), dp // 16
    zh, c = hd // 2, lax.rem(hd, 2)
    return x, y, zh * 4 + zl, c


def place(x, y, z, c):
    return ((y * 4 + lax.rem(z, 4)) * 4 + x, (z // 4) * 2 + c)


def wrap(a, n):
    return lax.rem(a + 4 * n, n)


def remote(src, dst, send_sem, recv_sem, device):
    return pltpu.make_async_remote_copy(
        src_ref=src,
        dst_ref=dst,
        send_sem=send_sem,
        recv_sem=recv_sem,
        device_id=device,
        device_id_type=MESH,
    )


class Peers:
    def __init__(self):
        self.x, self.y, self.z, self.c = coords()
        self.s = 2 * self.x + self.c
        x, y, z, c, s = self.x, self.y, self.z, self.c, self.s
        self.group = [wrap(s + d, 8) for d in range(1, 8)]
        self.group_dev = [place(g // 2, y, z, lax.rem(g, 2)) for g in self.group]
        self.sender = [wrap(s - d, 8) for d in range(1, 8)]
        self.y_dev = [place(x, wrap(y + d, 4), z, c) for d in range(1, 4)]
        self.up = place(x, y, wrap(z + 1, 16), c)
        self.down = place(x, y, wrap(z - 1, 16), c)
        self.up4 = place(x, y, wrap(z + 4, 16), c)
        self.down4 = place(x, y, wrap(z - 4, 16), c)
        self.z_near = [self.z_dev(k) for k in (1, -1, 2, -2, 4, -4, 8)]

    def z_dev(self, k):
        return place(self.x, self.y, wrap(self.z + k, 16), self.c)

    def signal_all(self):
        barrier = pltpu.get_barrier_semaphore()
        peers = [*self.group_dev, *self.y_dev, *self.z_near]
        for peer in peers:
            pl.semaphore_signal(barrier, inc=1, device_id=peer, device_id_type=MESH)
        return barrier, len(peers)


def head_sums(o_ref, do_ref, rows):
    lane = lax.broadcasted_iota(jnp.int32, (rows, D), 1)
    total = jnp.zeros((rows, D), F32)
    for g in range(8 * QPK):
        cols = slice(g * D, (g + 1) * D)
        one = jnp.sum(o_ref[:, cols].astype(F32) * do_ref[:, cols].astype(F32), axis=1, keepdims=True)
        total = jnp.where(lane == g, one, total)
    return total


def dot_t(a, b):
    return lax.dot_general(a, b, (((1,), (1,)), ((), ())), preferred_element_type=F32)


def dot(a, b):
    return lax.dot_general(a, b, (((1,), (0,)), ((), ())), preferred_element_type=F32)


def t_dot(a, b):
    return lax.dot_general(a, b, (((0,), (0,)), ((), ())), preferred_element_type=F32)


def grads(q, do, delta, k, v, bias, filled):
    scores = dot_t(q, k) * SCALE + bias
    highest = jnp.max(scores, axis=1, keepdims=True)
    e = jnp.exp(scores - highest)
    total = jnp.sum(e, axis=1, keepdims=True)
    likely = e * jnp.where(filled, 1.0 / total, 0.0)
    prob_grad = dot_t(do, v)
    score_grad = (likely * (prob_grad - delta)).astype(BF)
    dq = dot(score_grad, k) * SCALE
    dk = t_dot(score_grad, q) * SCALE
    dv = t_dot(likely.astype(BF), do)
    return dq, dk, dv


def main_kernel(
    rq, rk, rv, ro, rdo, pq, pk, pv, po, pdo, resp_len, resp_prompt, plan_rank, plan_offset,
    dq_o, dk_o, dv_o, pdq_in, pkv_in,
    ro_s, rdo_s, pq_s, pk_s, pv_s, po_s, pdo_s, tab_s, pkv_s, pqd_s, dl_s,
    rq_in, rdo_in, rkv, prev, g_in, pqd, dl,
    bias_s, filled_s, part, dq_s, cur, prev_d, pdq,
    back, y_out, y_in, own_sum, n_out, n_in, f_out, f_in, kv_s, pkvo_s,
    load_sem, a_send, a_recv, own_sem, sh_send, sh_recv,
    f_send, f_recv, n_send, n_recv, y_send, y_recv,
    ao_send, ao_recv, owno_sem, sho_send, sho_recv,
    fo_send, fo_recv, no_send, no_recv, yo_send, yo_recv,
):
    me = Peers()
    s, y, z = me.s, me.y, me.z
    barrier, count = me.signal_all()
    pairs = [(pk, pk_s), (pv, pv_s), (pq, pq_s), (pdo, pdo_s), (po, po_s), (ro, ro_s), (rdo, rdo_s)]
    loads = [pltpu.make_async_copy(src, dst, load_sem.at[n]) for n, (src, dst) in enumerate(pairs)]
    for load in loads:
        load.start()
    for n, table in enumerate((resp_len, resp_prompt, plan_rank, plan_offset)):
        loads.append(pltpu.make_async_copy(table, tab_s.at[n : n + 1], load_sem.at[7 + n]))
        loads[-1].start()
    loads[0].wait()
    loads[1].wait()
    for g in range(8):
        k8 = pk_s[:, g * D : (g + 1) * D].astype(F32)
        v8 = pv_s[:, g * D : (g + 1) * D].astype(F32)
        pkv_s[g] = jnp.concatenate([k8, v8], axis=0).astype(BF)
    pl.semaphore_wait(barrier, count)

    def masks():
        zh = z // 4
        tab_s[4:8, :] = jnp.zeros((4, 256), jnp.int32)
        tab_row = tab_s[...].astype(F32)
        tab_col = tab_row.T

        def one(r, _):
            rank = ((y * 4 + lax.rem(z, 4)) * 4 + r).astype(F32)
            base = zh * 64
            holding = tab_row[2:3, :] == rank
            owner = tab_row[1:2, :]
            first = jnp.min(jnp.where(holding, owner, 16.0), axis=1, keepdims=True)
            last = jnp.max(jnp.where(holding, owner, 0.0), axis=1, keepdims=True)
            row = (lax.broadcasted_iota(jnp.int32, (64, PROMPT), 0) + base).astype(F32)
            label = (lax.broadcasted_iota(jnp.int32, (64, PROMPT), 1) + 1).astype(F32)
            start, stop = tab_row[3:4, :], tab_row[3:4, :] + tab_row[0:1, :]
            member = holding & (row >= start) & (row < stop)
            seg_q = jnp.sum(jnp.where(member, label, 0.0), axis=1, keepdims=True)
            owner_q = jnp.sum(jnp.where(member, jnp.broadcast_to(owner, member.shape), 0.0), axis=1, keepdims=True)
            key_row = (lax.broadcasted_iota(jnp.int32, (PROMPT, D), 1) + base - 64).astype(F32)
            key_label = (lax.broadcasted_iota(jnp.int32, (PROMPT, D), 0) + 1).astype(F32)
            start_c, stop_c = tab_col[:, 3:4], tab_col[:, 3:4] + tab_col[:, 0:1]
            key_member = (tab_col[:, 2:3] == rank) & (key_row >= start_c) & (key_row < stop_c)
            seg_k = jnp.sum(jnp.where(key_member, key_label, 0.0), axis=0, keepdims=True)
            filled = seg_q > 0.0
            q_pos = lax.broadcasted_iota(jnp.int32, (64, D), 0) + 64
            k_pos = lax.broadcasted_iota(jnp.int32, (64, D), 1)
            own = (seg_q == seg_k) & filled & (k_pos <= q_pos)
            take_first = filled & (owner_q == first)
            take_last = filled & (owner_q == last) & (first != last)
            bias_s[r, :, 0:256] = jnp.broadcast_to(jnp.where(take_first, 0.0, MASKED), (64, PROMPT))
            bias_s[r, :, 256:512] = jnp.broadcast_to(jnp.where(take_last, 0.0, MASKED), (64, PROMPT))
            bias_s[r, :, 512:640] = jnp.where(own, 0.0, MASKED)
            filled_s[r] = jnp.broadcast_to(jnp.where(filled, 1.0, 0.0), (64, D))
            return 0

        lax.fori_loop(0, 4, one, 0)

    def prompts_of(r):
        rank = ((y * 4 + lax.rem(z, 4)) * 4 + r).astype(F32)
        table = tab_s[0:4, :].astype(F32)
        holding = table[2:3, :] == rank
        owner = table[1:2, :]
        first = jnp.min(jnp.where(holding, owner, 15.0))
        last = jnp.max(jnp.where(holding, owner, 0.0))
        return jnp.clip(first.astype(jnp.int32), 0, 15), jnp.clip(last.astype(jnp.int32), 0, 15)

    def stack(parts):
        return jnp.concatenate(parts, axis=0)

    def prompt_rows(p):
        kv = g_in[p].reshape(32, 16, D).astype(F32)
        return kv[:, 0:8, :].reshape(PROMPT, D).astype(BF), kv[:, 8:16, :].reshape(PROMPT, D).astype(BF)

    def keep(n, dk, dv):
        part[n, :, 0:8, :] = dk.reshape(32, 8, D)
        part[n, :, 8:16, :] = dv.reshape(32, 8, D)

    def lead_grads():
        p, zh = y * 4 + lax.rem(z, 4), z // 4
        lead = pqd[...].astype(F32)
        q = stack([lead[:, i * 8 : i * 8 + 8, :].reshape(64, D) for i in range(QPK)]).astype(BF)
        do = stack([lead[:, (i + 5) * 8 : (i + 5) * 8 + 8, :].reshape(64, D) for i in range(QPK)]).astype(BF)
        dls = [dl[j].T for j in range(8)]
        delta = stack([dls[j][32:40, i : i + 1] for i in range(QPK) for j in range(8)])

        def place_of(n, hi):
            j, i = (n // 8) % 8, n % 8
            return (j // 2) * 64 + (hi * 2 + j % 2) * 8 + i

        n_q = lax.broadcasted_iota(jnp.int32, (64, PROMPT), 0)
        n_k = lax.broadcasted_iota(jnp.int32, (64, PROMPT), 1)
        bias = jnp.where(place_of(n_k, n_k // 64) <= place_of(n_q, zh), 0.0, MASKED)
        k, v = prompt_rows(p)
        dq, dk, dv = grads(q, do, delta, k, v, stack([bias] * QPK), True)
        keep(8, dk, dv)
        for j in range(8):
            tiles = [dq[i * 64 + j * 8 : i * 64 + j * 8 + 8] for i in range(QPK)]
            pdq[j] = stack([*tiles, jnp.zeros((8, D), F32)]).astype(BF)

    def cols(ref, h, width):
        return ref.at[:, pl.ds(pl.multiple_of(h * width, D), width)]

    mine = (y * 4 + lax.rem(z, 4), z // 4)
    sources = [
        lambda h: pkv_s.at[h],
        lambda h: cols(rk, h, D),
        lambda h: cols(rv, h, D),
        lambda h: pqd_s.at[h],
        lambda h: cols(rq, h, W),
        lambda h: cols(rdo, h, W),
        lambda h: dl_s.at[h],
    ]
    landing = [
        lambda j: g_in.at[mine[0], mine[1], j],
        lambda j: rkv.at[0, j],
        lambda j: rkv.at[1, j],
        lambda j: pqd.at[j],
        lambda j: rq_in.at[j],
        lambda j: rdo_in.at[j],
        lambda j: dl.at[j],
    ]
    kinds = len(sources)
    own = [pltpu.make_async_copy(sources[n](s), landing[n](s), own_sem.at[n]) for n in range(kinds)]
    sent = []

    def send(n):
        own[n].start()
        for d in range(7):
            h = me.group[d]
            copy = remote(sources[n](h), landing[n](s), a_send.at[n, d], a_recv.at[n, s], me.group_dev[d])
            copy.start()
            sent.append(copy)

    def arrived(n):
        own[n].wait()
        for d in range(7):
            j = me.sender[d]
            remote(landing[n](j), landing[n](j), a_send.at[n, d], a_recv.at[n, j], me.group_dev[d]).wait_recv()

    send(0)
    send(1)
    send(2)
    send(4)
    send(5)
    loads[2].wait()
    loads[3].wait()
    for g in range(8):
        parts = [pq_s[:, (g * QPK + i) * D : (g * QPK + i + 1) * D].astype(F32) for i in range(QPK)]
        parts += [pdo_s[:, (g * QPK + i) * D : (g * QPK + i + 1) * D].astype(F32) for i in range(QPK)]
        pqd_s[g] = jnp.concatenate(parts, axis=0).astype(BF)
    send(3)

    def block(yy, zz):
        return g_in.at[yy * 4 + lax.rem(zz, 4), zz // 4]

    def at(k, m):
        return wrap(z + STEP[k] + NEAR[m], 16)

    def across(k, m):
        there = block(y, at(k, m))
        for d in range(3):
            copy = remote(there, there, y_send.at[4 * k + m, d], y_recv.at[4 * k + m, d], me.y_dev[d])
            copy.start()
            sent.append(copy)

    def along(k, m):
        there = block(y, at(k, 0))
        return remote(there, there, n_send.at[k, m - 1], n_recv.at[k, m - 1], me.z_dev(-NEAR[m]))

    def far(k):
        there = block(y, z)
        return remote(there, there, f_send.at[k - 1], f_recv.at[k - 1], me.z_dev(-STEP[k]))

    def spread(k):
        if k > 0:
            there = block(y, at(k, 0))
            remote(there, there, f_send.at[k - 1], f_recv.at[k - 1], me.up).wait_recv()
        for m in (1, 2, 3):
            copy = along(k, m)
            copy.start()
            sent.append(copy)
        across(k, 0)

    def pass_on(k):
        for m in (1, 2, 3):
            there = block(y, at(k, m))
            remote(there, there, n_send.at[k, m - 1], n_recv.at[k, m - 1], me.up).wait_recv()
            across(k, m)

    arrived(0)
    for k in (3, 1, 2):
        copy = far(k)
        copy.start()
        sent.append(copy)
    spread(0)
    for load in loads[4:]:
        load.wait()
    sums = [head_sums(ro_s, rdo_s, 32), head_sums(po_s, pdo_s, 8), jnp.zeros((D - 40, D), F32)]
    sums = jnp.concatenate(sums, axis=0).T
    for g in range(8):
        dl_s[g, 0:QPK, :] = sums[g * QPK : (g + 1) * QPK, :]
        dl_s[g, QPK:8, :] = jnp.zeros((8 - QPK, D), F32)
    send(6)
    masks()
    pass_on(0)
    arrived(1)
    arrived(2)
    shift = remote(rkv, prev, sh_send, sh_recv, me.up4)
    shift.start()
    spread(1)
    spread(2)
    pass_on(1)
    pass_on(2)
    spread(3)
    pass_on(3)
    for n in range(3, kinds):
        arrived(n)
    lead_grads()
    shift.wait()
    for k in range(4):
        for m in range(4):
            for d in range(3):
                there = block(wrap(y - d - 1, 4), at(k, m))
                remote(there, there, y_send.at[4 * k + m, d], y_recv.at[4 * k + m, d], me.y_dev[d]).wait_recv()


    def rank_grads(r, _):
        first, last = prompts_of(r)
        bias = stack([bias_s[r]] * QPK)
        filled = stack([filled_s[r, :, 0:1]] * QPK) > 0.0
        two = pl.ds(2 * r, 2)
        q2 = rq_in[two].reshape(64, W)
        do2 = rdo_in[two].reshape(64, W)
        q = stack([q2[:, i * D : (i + 1) * D] for i in range(QPK)])
        do = stack([do2[:, i * D : (i + 1) * D] for i in range(QPK)])
        dl2 = dl[two]
        dl0, dl1 = dl2[0].T, dl2[1].T
        delta = stack([half[0:32, i : i + 1] for i in range(QPK) for half in (dl0, dl1)])
        k1, v1 = prompt_rows(first)
        k2, v2 = prompt_rows(last)
        k = stack([k1, k2, prev[0, two].reshape(64, D), rkv[0, two].reshape(64, D)])
        v = stack([v1, v2, prev[1, two].reshape(64, D), rkv[1, two].reshape(64, D)])
        dq, dk, dv = grads(q, do, delta, k, v, bias, filled)
        dq = dq.astype(BF)
        dq_s[two] = jnp.concatenate([dq[i * 64 : (i + 1) * 64] for i in range(QPK)], axis=1).reshape(2, 32, W)
        keep(2 * r, dk[0:256], dv[0:256])
        keep(2 * r + 1, dk[256:512], dv[256:512])
        prev_d[0, two] = dk[512:576].astype(BF).reshape(2, 32, D)
        prev_d[1, two] = dv[512:576].astype(BF).reshape(2, 32, D)
        cur[0, two] = dk[576:640].reshape(2, 32, D)
        cur[1, two] = dv[576:640].reshape(2, 32, D)
        return 0

    lax.fori_loop(0, 4, rank_grads, 0)

    owners = [prompts_of(jnp.int32(r)) for r in range(4)]
    part[9] = jnp.zeros((32, 16, D), F32)

    def summed(yy, zz):
        p, rows = yy * 4 + lax.rem(zz, 4), pl.ds(zz // 4 * 8, 8)
        total = None
        for r, (first, last) in enumerate(owners):
            n = jnp.where(first == p, 2 * r, jnp.where(last == p, 2 * r + 1, 9))
            total = part[n, rows] if total is None else total + part[n, rows]
        return total

    def y_copy(k, m, d):
        n = 4 * k + m
        return remote(y_out.at[d, n], y_in.at[d, n], yo_send.at[n, d], yo_recv.at[n, d], me.y_dev[d])

    def exchange(k):
        for m in (1, 2, 3, 0):
            for d in range(3):
                y_out[d, 4 * k + m] = summed(wrap(y + d + 1, 4), at(k, m)).astype(BF)
                copy = y_copy(k, m, d)
                copy.start()
                sent.append(copy)

    exchange(3)
    shift_back = remote(prev_d, back, sho_send, sho_recv, me.down4)
    shift_back.start()
    exchange(1)
    exchange(2)
    exchange(0)

    out_sources = [
        lambda h: dq_s.at[h],
        lambda h: pdq.at[h],
        lambda h: kv_s.at[0, h],
        lambda h: kv_s.at[1, h],
        lambda h: pkvo_s.at[h],
    ]
    out_landing = [
        lambda j: cols(dq_o, j, W),
        lambda j: pdq_in.at[j],
        lambda j: cols(dk_o, j, D),
        lambda j: cols(dv_o, j, D),
        lambda j: pkv_in.at[j],
    ]
    out_own = {}

    def give(n):
        out_own[n] = pltpu.make_async_copy(out_sources[n](s), out_landing[n](s), owno_sem.at[n])
        out_own[n].start()
        for d in range(7):
            h = me.group[d]
            copy = remote(out_sources[n](h), out_landing[n](s), ao_send.at[n, d], ao_recv.at[n, s], me.group_dev[d])
            copy.start()
            sent.append(copy)

    def taken(n):
        out_own[n].wait()
        for d in range(7):
            j = me.sender[d]
            remote(out_landing[n](j), out_landing[n](j), ao_send.at[n, d], ao_recv.at[n, j], me.group_dev[d]).wait_recv()

    give(0)
    give(1)

    def partial(k, m):
        total = summed(y, at(k, m))
        if m == 0:
            total += part[8, pl.ds(at(k, m) // 4 * 8, 8)]
        for d in range(3):
            y_copy(k, m, d).wait_recv()
            total += y_in[d, 4 * k + m].astype(F32)
        return total

    def n_copy(k, m):
        n = (k, m - 1)
        return remote(n_out.at[*n], n_in.at[*n], no_send.at[*n], no_recv.at[*n], me.z_dev(NEAR[m]))

    def f_copy(k):
        n = k - 1
        return remote(f_out.at[n], f_in.at[n], fo_send.at[n], fo_recv.at[n], me.z_dev(STEP[k]))

    def collect(k):
        for m in (1, 2, 3):
            n_out[k, m - 1] = partial(k, m).astype(BF)
            copy = n_copy(k, m)
            copy.start()
            sent.append(copy)
        own_sum[k] = partial(k, 0)

    def finish(k):
        total = own_sum[k]
        for m in (1, 2, 3):
            n_copy(k, m).wait_recv()
            total += n_in[k, m - 1].astype(F32)
        if k > 0:
            f_out[k - 1] = total.astype(BF)
            copy = f_copy(k)
            copy.start()
            sent.append(copy)
        return total

    collect(3)
    collect(1)
    finish(3)
    collect(2)
    finish(1)
    shift_back.wait_recv()
    kv_s[...] = (cur[...] + back[...].astype(F32)).astype(BF)
    give(2)
    give(3)
    collect(0)
    finish(2)
    total = finish(0)
    for k in (1, 2, 3):
        f_copy(k).wait_recv()
        total += f_in[k - 1].astype(F32)
    pkvo_s[...] = total.astype(BF)
    give(4)
    for n in (1, 0, 2, 3, 4):
        taken(n)
    shift_back.wait_send()
    for copy in sent:
        copy.wait_send()


def finish_kernel(dq, dk, dv, pdq, pkv, dq_o, dk_o, dv_o, pdq_o, pdk_o, pdv_o):
    dq_o[...] = dq[...]
    dk_o[...] = dk[...]
    dv_o[...] = dv[...]
    for h in range(8):
        tiles = pdq[h].astype(F32)
        for i in range(QPK):
            pdq_o[:, (h * QPK + i) * D : (h * QPK + i + 1) * D] = tiles[i * 8 : i * 8 + 8].astype(BF)
        tile = pkv[h].astype(F32)
        pdk_o[:, h * D : (h + 1) * D] = tile[0:8].astype(BF)
        pdv_o[:, h * D : (h + 1) * D] = tile[8:16].astype(BF)


def vmem(n):
    return [pl.BlockSpec(memory_space=pltpu.VMEM)] * n


def shapes(*items):
    return [jax.ShapeDtypeStruct(shape, dtype) for shape, dtype in items]


def local(*args):
    dma = pltpu.SemaphoreType.DMA
    rows, tables = args[:10], [table.reshape(1, 256) for table in args[10:]]
    bf = lambda *shape: pltpu.VMEM(shape, BF)
    f32 = lambda *shape: pltpu.VMEM(shape, F32)
    landed = pl.pallas_call(
        main_kernel,
        out_shape=shapes(
            ((32, 40 * D), BF), ((32, 8 * D), BF), ((32, 8 * D), BF), ((8, 48, D), BF), ((8, 16, D), BF)
        ),
        in_specs=[pl.BlockSpec(memory_space=pl.ANY)] * 14,
        out_specs=vmem(5),
        scratch_shapes=[
            bf(32, 40 * D), bf(32, 40 * D), bf(8, 40 * D), bf(8, 8 * D), bf(8, 8 * D), bf(8, 40 * D), bf(8, 40 * D),
            pltpu.VMEM((8, 256), jnp.int32), bf(8, 16, D), bf(8, 80, D), f32(8, 8, D),
            bf(8, 32, W), bf(8, 32, W), bf(2, 8, 32, D), bf(2, 8, 32, D), bf(16, 4, 8, 16, D), bf(8, 80, D), f32(8, 8, D),
            f32(4, 64, 640), f32(4, 64, D), f32(10, 32, 16, D), bf(8, 32, W), f32(2, 8, 32, D), bf(2, 8, 32, D), bf(8, 48, D),
            bf(2, 8, 32, D), bf(3, 16, 8, 16, D), bf(3, 16, 8, 16, D), f32(4, 8, 16, D), bf(4, 3, 8, 16, D), bf(4, 3, 8, 16, D),
            bf(3, 8, 16, D), bf(3, 8, 16, D), bf(2, 8, 32, D), bf(8, 16, D),
            dma((11,)), dma((7, 7)), dma((7, 8)), dma((7,)), dma, dma,
            dma((3,)), dma((3,)), dma((4, 3)), dma((4, 3)), dma((16, 3)), dma((16, 3)),
            dma((5, 7)), dma((5, 8)), dma((5,)), dma, dma,
            dma((3,)), dma((3,)), dma((4, 3)), dma((4, 3)), dma((16, 3)), dma((16, 3)),
        ],
        compiler_params=pltpu.CompilerParams(collective_id=0, has_side_effects=True, vmem_limit_bytes=60 * 2**20),
        name="exchange_and_grads",
    )(*rows, *tables)
    return tuple(
        pl.pallas_call(
            finish_kernel,
            out_shape=shapes(
                ((32, 40 * D), BF), ((32, 8 * D), BF), ((32, 8 * D), BF),
                ((8, 40 * D), BF), ((8, 8 * D), BF), ((8, 8 * D), BF),
            ),
            in_specs=vmem(5),
            out_specs=vmem(6),
            name="finish",
        )(*landed)
    )


def solution(mesh):
    rows = P(("dp", "head"), None)
    return jax.shard_map(
        local,
        mesh=mesh,
        in_specs=(rows,) * 10 + (P(),) * 4,
        out_specs=(rows,) * 6,
        check_vma=False,
    )
```

time: 122 us -> 104 us (0.85)
  local copies, waits for them, and re-layouts: 13.3 us -> 0 us
  Pallas kernels: 107 us -> 103 us
    unnamed x26 -> x0, local copies, waits for them, and re-layouts: 12.5 us -> none
    pallas_call x3 -> x2, Pallas kernels: 107 us -> 103 us  [the longest x1 101 us: local(): pl.pallas_call(main_kernel, out_shape=shapes(((32, 40 * D), BF), ((32, 8...]
where the time goes in v2:
time: 104 us; the launch traced here: 103 us
  Pallas kernels  103 us (99%)
    pallas_call x1, Pallas kernels, local(): pl.pallas_call(main_kernel, out_shape=shapes(((32, 40 * D), BF), ((32, 8...  101 us

profile of v2, /device:TPU:1, one launch (start us, length us, event | category | flops | bytes accessed | tf_op | source)
XLA Modules:
  0.0 103.3 jit_solution(6119259430615212516)
XLA Ops:
  0.6 100.8 %exchange_and_grads.1 = (bf16[32,5120]{1,0:T(8,128)(2,1)}, bf16[32,1024]{1,0:T(8,128)(2,1)}, bf16[32,1024]{1,0:T(8,128)(2,1)}, bf16[8,48,128]{2,1,0:T(8,128)(2,1)}, bf16[8,16,128]{2,1,0:T(8,128)(2,1)}) custom-call(bf16[32,5120]{1,0:T(8,128)(2,1)} %rq.1, bf16[32,1024]{1,0:T(8,128)(2,1)} %rk.1, bf16[32,1024]{1,0:T(8,128)(2,1)} %rv.1, bf16[32,5120]{1,0:T(8,128)(2,1)} %ro.1, ...), custom_call_target="tpu_custom_call" | custom-call | tf_op jit(solution)/shard_map/exchange_and_grads/pallas_call | solution.py:527
  101.5 1.9 %finish.1 = (bf16[32,5120]{1,0:T(8,128)(2,1)}, bf16[32,1024]{1,0:T(8,128)(2,1)}, bf16[32,1024]{1,0:T(8,128)(2,1)}, bf16[8,5120]{1,0:T(8,128)(2,1)}, bf16[8,1024]{1,0:T(8,128)(2,1)}, /*index=5*/bf16[8,1024]{1,0:T(8,128)(2,1)}) custom-call(bf16[32,5120]{1,0:T(8,128)(2,1)} %get-tuple-element.11.dq, bf16[32,1024]{1,0:T(8,128)(2,1)} %get-tuple-element.12.dk, ...), custom_call_target="tpu_custom_call" | custom-call | tf_op jit(solution)/shard_map/finish/pallas_call | solution.py:550

commit v3 on v2

--- a/solution.py
+++ b/solution.py
@@ -11,8 +11,8 @@
 PROMPT = 256
 MASKED = -1e30
 SCALE = D**-0.5
-STEP = (0, 4, -4, 8)
-NEAR = (0, 1, 2, -1)
+STEP = (4, 8, -4, 0)
+NEAR = (1, 2, -1, 0)
 MESH = pl.DeviceIdType.MESH
 BF = jnp.bfloat16
 F32 = jnp.float32
@@ -54,11 +54,7 @@
         self.group_dev = [place(g // 2, y, z, lax.rem(g, 2)) for g in self.group]
         self.sender = [wrap(s - d, 8) for d in range(1, 8)]
         self.y_dev = [place(x, wrap(y + d, 4), z, c) for d in range(1, 4)]
-        self.up = place(x, y, wrap(z + 1, 16), c)
-        self.down = place(x, y, wrap(z - 1, 16), c)
-        self.up4 = place(x, y, wrap(z + 4, 16), c)
-        self.down4 = place(x, y, wrap(z - 4, 16), c)
-        self.z_near = [self.z_dev(k) for k in (1, -1, 2, -2, 4, -4, 8)]
+        self.z_near = [self.z_dev(k) for k in (1, -1, 2, -2)]
 
     def z_dev(self, k):
         return place(self.x, self.y, wrap(self.z + k, 16), self.c)
@@ -111,7 +107,7 @@
     rq, rk, rv, ro, rdo, pq, pk, pv, po, pdo, resp_len, resp_prompt, plan_rank, plan_offset,
     dq_o, dk_o, dv_o, pdq_in, pkv_in,
     ro_s, rdo_s, pq_s, pk_s, pv_s, po_s, pdo_s, tab_s, pkv_s, pqd_s, dl_s,
-    rq_in, rdo_in, rkv, prev, g_in, pqd, dl,
+    rq_in, rdo_in, rkv, via, prev, g_in, pqd, dl,
     bias_s, filled_s, part, dq_s, cur, prev_d, pdq,
     back, y_out, y_in, own_sum, n_out, n_in, f_out, f_in, kv_s, pkvo_s,
     load_sem, a_send, a_recv, own_sem, sh_send, sh_recv,
@@ -273,46 +269,36 @@
     def block(yy, zz):
         return g_in.at[yy * 4 + lax.rem(zz, 4), zz // 4]
 
-    def at(k, m):
-        return wrap(z + STEP[k] + NEAR[m], 16)
-
-    def across(k, m):
-        there = block(y, at(k, m))
+    def moved(k):
+        return block(y, wrap(z + k, 16))
+
+    def across(k):
+        n = k + 8
         for d in range(3):
-            copy = remote(there, there, y_send.at[4 * k + m, d], y_recv.at[4 * k + m, d], me.y_dev[d])
+            copy = remote(moved(k), moved(k), y_send.at[n, d], y_recv.at[n, d], me.y_dev[d])
             copy.start()
-            sent.append(copy)
-
-    def along(k, m):
-        there = block(y, at(k, 0))
-        return remote(there, there, n_send.at[k, m - 1], n_recv.at[k, m - 1], me.z_dev(-NEAR[m]))
-
-    def far(k):
-        there = block(y, z)
-        return remote(there, there, f_send.at[k - 1], f_recv.at[k - 1], me.z_dev(-STEP[k]))
-
-    def spread(k):
-        if k > 0:
-            there = block(y, at(k, 0))
-            remote(there, there, f_send.at[k - 1], f_recv.at[k - 1], me.up).wait_recv()
-        for m in (1, 2, 3):
-            copy = along(k, m)
-            copy.start()
-            sent.append(copy)
-        across(k, 0)
-
-    def pass_on(k):
-        for m in (1, 2, 3):
-            there = block(y, at(k, m))
-            remote(there, there, n_send.at[k, m - 1], n_recv.at[k, m - 1], me.up).wait_recv()
-            across(k, m)
-
-    arrived(0)
-    for k in (3, 1, 2):
-        copy = far(k)
+
+    def two(t, sign):
+        n = t if sign > 0 else 4 + t
+        return remote(moved(-2 * sign * t), moved(-2 * sign * t), f_send.at[n], f_recv.at[n], me.z_dev(2 * sign))
+
+    def one(t, sign):
+        n = t if sign > 0 else 4 + t
+        return remote(moved(-2 * sign * t), moved(-2 * sign * t), n_send.at[n], n_recv.at[n], me.z_dev(sign))
+
+    def came(copy):
+        copy.wait_recv()
+
+    def go(copy):
         copy.start()
         sent.append(copy)
-    spread(0)
+
+    arrived(0)
+    go(two(0, 1))
+    go(two(0, -1))
+    go(one(0, 1))
+    go(one(0, -1))
+    across(0)
     for load in loads[4:]:
         load.wait()
     sums = [head_sums(ro_s, rdo_s, 32), head_sums(po_s, pdo_s, 8), jnp.zeros((D - 40, D), F32)]
@@ -322,27 +308,45 @@
         dl_s[g, QPK:8, :] = jnp.zeros((8 - QPK, D), F32)
     send(6)
     masks()
-    pass_on(0)
-    arrived(1)
-    arrived(2)
-    shift = remote(rkv, prev, sh_send, sh_recv, me.up4)
-    shift.start()
-    spread(1)
-    spread(2)
-    pass_on(1)
-    pass_on(2)
-    spread(3)
-    pass_on(3)
+    for t in range(5):
+        if t > 0:
+            came(two(t - 1, 1))
+            if t < 4:
+                go(two(t, 1))
+                go(one(t, 1))
+                came(two(t - 1, -1))
+                if t < 3:
+                    go(two(t, -1))
+                go(one(t, -1))
+                across(2 * t)
+            across(-2 * t)
+        if t == 1:
+            arrived(1)
+            arrived(2)
+            shift = remote(rkv, via, sh_send.at[0], sh_recv.at[0], me.z_dev(2))
+            go(shift)
+        if t < 4:
+            came(one(t, -1))
+            across(1 + 2 * t)
+            came(one(t, 1))
+            across(-1 - 2 * t)
+        if t == 3:
+            shift.wait_recv()
+            shift = remote(via, prev, sh_send.at[1], sh_recv.at[1], me.z_dev(2))
+            go(shift)
     for n in range(3, kinds):
         arrived(n)
     lead_grads()
-    shift.wait()
-    for k in range(4):
-        for m in range(4):
-            for d in range(3):
-                there = block(wrap(y - d - 1, 4), at(k, m))
-                remote(there, there, y_send.at[4 * k + m, d], y_recv.at[4 * k + m, d], me.y_dev[d]).wait_recv()
-
+    shift.wait_recv()
+
+    def settle(n, _):
+        for d in range(3):
+            there = block(wrap(y - d - 1, 4), wrap(z + n - 8, 16))
+            remote(there, there, y_send.at[n, d], y_recv.at[n, d], me.y_dev[d]).wait_recv()
+            remote(moved(0), moved(0), y_send.at[n, d], y_recv.at[n, d], me.y_dev[d]).wait_send()
+        return 0
+
+    lax.fori_loop(0, 16, settle, 0)
 
     def rank_grads(r, _):
         first, last = prompts_of(r)
@@ -384,24 +388,24 @@
             total = part[n, rows] if total is None else total + part[n, rows]
         return total
 
-    def y_copy(k, m, d):
-        n = 4 * k + m
+    def at(k, m):
+        return wrap(z + STEP[k] + NEAR[m], 16)
+
+    def y_copy(n, d):
         return remote(y_out.at[d, n], y_in.at[d, n], yo_send.at[n, d], yo_recv.at[n, d], me.y_dev[d])
 
-    def exchange(k):
-        for m in (1, 2, 3, 0):
-            for d in range(3):
-                y_out[d, 4 * k + m] = summed(wrap(y + d + 1, 4), at(k, m)).astype(BF)
-                copy = y_copy(k, m, d)
-                copy.start()
-                sent.append(copy)
-
-    exchange(3)
-    shift_back = remote(prev_d, back, sho_send, sho_recv, me.down4)
+    def exchange(n, _):
+        m = lax.rem(n, 4) + 1
+        zz = wrap(z + 4 * (n // 4 + 1) + m - 4 * (m // 3), 16)
+        for d in range(3):
+            y_out[d, n] = summed(wrap(y + d + 1, 4), zz).astype(BF)
+            y_copy(n, d).start()
+        return 0
+
+    lax.fori_loop(0, 4, exchange, 0)
+    shift_back = remote(prev_d, back, sho_send, sho_recv, me.z_dev(-4))
     shift_back.start()
-    exchange(1)
-    exchange(2)
-    exchange(0)
+    lax.fori_loop(4, 16, exchange, 0)
 
     out_sources = [
         lambda h: dq_s.at[h],
@@ -439,56 +443,50 @@
 
     def partial(k, m):
         total = summed(y, at(k, m))
-        if m == 0:
+        if m == 3:
             total += part[8, pl.ds(at(k, m) // 4 * 8, 8)]
         for d in range(3):
-            y_copy(k, m, d).wait_recv()
+            y_copy(4 * k + m, d).wait_recv()
             total += y_in[d, 4 * k + m].astype(F32)
         return total
 
     def n_copy(k, m):
-        n = (k, m - 1)
-        return remote(n_out.at[*n], n_in.at[*n], no_send.at[*n], no_recv.at[*n], me.z_dev(NEAR[m]))
+        return remote(n_out.at[k, m], n_in.at[k, m], no_send.at[k, m], no_recv.at[k, m], me.z_dev(NEAR[m]))
 
     def f_copy(k):
-        n = k - 1
-        return remote(f_out.at[n], f_in.at[n], fo_send.at[n], fo_recv.at[n], me.z_dev(STEP[k]))
+        return remote(f_out.at[k], f_in.at[k], fo_send.at[k], fo_recv.at[k], me.z_dev(STEP[k]))
 
     def collect(k):
-        for m in (1, 2, 3):
-            n_out[k, m - 1] = partial(k, m).astype(BF)
-            copy = n_copy(k, m)
-            copy.start()
-            sent.append(copy)
-        own_sum[k] = partial(k, 0)
+        for m in range(3):
+            n_out[k, m] = partial(k, m).astype(BF)
+            go(n_copy(k, m))
+        own_sum[k] = partial(k, 3)
 
     def finish(k):
         total = own_sum[k]
-        for m in (1, 2, 3):
-            n_copy(k, m).wait_recv()
-            total += n_in[k, m - 1].astype(F32)
-        if k > 0:
-            f_out[k - 1] = total.astype(BF)
-            copy = f_copy(k)
-            copy.start()
-            sent.append(copy)
+        for m in range(3):
+            came(n_copy(k, m))
+            total += n_in[k, m].astype(F32)
+        if k < 3:
+            f_out[k] = total.astype(BF)
+            go(f_copy(k))
         return total
 
-    collect(3)
+    collect(0)
     collect(1)
-    finish(3)
+    finish(0)
     collect(2)
     finish(1)
     shift_back.wait_recv()
     kv_s[...] = (cur[...] + back[...].astype(F32)).astype(BF)
     give(2)
     give(3)
-    collect(0)
+    collect(3)
     finish(2)
-    total = finish(0)
-    for k in (1, 2, 3):
-        f_copy(k).wait_recv()
-        total += f_in[k - 1].astype(F32)
+    total = finish(3)
+    for k in range(3):
+        came(f_copy(k))
+        total += f_in[k].astype(F32)
     pkvo_s[...] = total.astype(BF)
     give(4)
     for n in (1, 0, 2, 3, 4):
@@ -496,6 +494,13 @@
     shift_back.wait_send()
     for copy in sent:
         copy.wait_send()
+
+    def leave(n, _):
+        for d in range(3):
+            y_copy(n, d).wait_send()
+        return 0
+
+    lax.fori_loop(0, 16, leave, 0)
 
 
 def finish_kernel(dq, dk, dv, pdq, pkv, dq_o, dk_o, dv_o, pdq_o, pdk_o, pdv_o):
@@ -534,12 +539,12 @@
         scratch_shapes=[
             bf(32, 40 * D), bf(32, 40 * D), bf(8, 40 * D), bf(8, 8 * D), bf(8, 8 * D), bf(8, 40 * D), bf(8, 40 * D),
             pltpu.VMEM((8, 256), jnp.int32), bf(8, 16, D), bf(8, 80, D), f32(8, 8, D),
-            bf(8, 32, W), bf(8, 32, W), bf(2, 8, 32, D), bf(2, 8, 32, D), bf(16, 4, 8, 16, D), bf(8, 80, D), f32(8, 8, D),
+            bf(8, 32, W), bf(8, 32, W), bf(2, 8, 32, D), bf(2, 8, 32, D), bf(2, 8, 32, D), bf(16, 4, 8, 16, D), bf(8, 80, D), f32(8, 8, D),
             f32(4, 64, 640), f32(4, 64, D), f32(10, 32, 16, D), bf(8, 32, W), f32(2, 8, 32, D), bf(2, 8, 32, D), bf(8, 48, D),
             bf(2, 8, 32, D), bf(3, 16, 8, 16, D), bf(3, 16, 8, 16, D), f32(4, 8, 16, D), bf(4, 3, 8, 16, D), bf(4, 3, 8, 16, D),
             bf(3, 8, 16, D), bf(3, 8, 16, D), bf(2, 8, 32, D), bf(8, 16, D),
-            dma((11,)), dma((7, 7)), dma((7, 8)), dma((7,)), dma, dma,
-            dma((3,)), dma((3,)), dma((4, 3)), dma((4, 3)), dma((16, 3)), dma((16, 3)),
+            dma((11,)), dma((7, 7)), dma((7, 8)), dma((7,)), dma((2,)), dma((2,)),
+            dma((7,)), dma((7,)), dma((8,)), dma((8,)), dma((16, 3)), dma((16, 3)),
             dma((5, 7)), dma((5, 8)), dma((5,)), dma, dma,
             dma((3,)), dma((3,)), dma((4, 3)), dma((4, 3)), dma((16, 3)), dma((16, 3)),
         ],

time: 104 us -> 90.9 us (0.87)
  Pallas kernels: 103 us -> 90.1 us
    pallas_call x1, Pallas kernels: 101 us -> 88.2 us  [local(): pl.pallas_call(main_kernel, out_shape=shapes(((32, 40 * D), BF), ((32, 8...]
where the time goes in v3:
time: 90.9 us; the launch traced here: 90.7 us
  Pallas kernels  90.1 us (99%)
    pallas_call x1, Pallas kernels, local(): pl.pallas_call(main_kernel, out_shape=shapes(((32, 40 * D), BF), ((32, 8...  88.2 us
    pallas_call x1, Pallas kernels, local(): pl.pallas_call(finish_kernel, out_shape=shapes(((32, 40 * D), BF), ((32,...  1.87 us

profile of v3, /device:TPU:1, one launch (start us, length us, event | category | flops | bytes accessed | tf_op | source)
XLA Modules:
  0.0 90.7 jit_solution(10166636670371411485)
XLA Ops:
  0.6 88.2 %exchange_and_grads.1 = (bf16[32,5120]{1,0:T(8,128)(2,1)}, bf16[32,1024]{1,0:T(8,128)(2,1)}, bf16[32,1024]{1,0:T(8,128)(2,1)}, bf16[8,48,128]{2,1,0:T(8,128)(2,1)}, bf16[8,16,128]{2,1,0:T(8,128)(2,1)}) custom-call(bf16[32,5120]{1,0:T(8,128)(2,1)} %rq.1, bf16[32,1024]{1,0:T(8,128)(2,1)} %rk.1, bf16[32,1024]{1,0:T(8,128)(2,1)} %rv.1, bf16[32,5120]{1,0:T(8,128)(2,1)} %ro.1, ...), custom_call_target="tpu_custom_call" | custom-call | tf_op jit(solution)/shard_map/exchange_and_grads/pallas_call | solution.py:532
  88.8 1.9 %finish.1 = (bf16[32,5120]{1,0:T(8,128)(2,1)}, bf16[32,1024]{1,0:T(8,128)(2,1)}, bf16[32,1024]{1,0:T(8,128)(2,1)}, bf16[8,5120]{1,0:T(8,128)(2,1)}, bf16[8,1024]{1,0:T(8,128)(2,1)}, /*index=5*/bf16[8,1024]{1,0:T(8,128)(2,1)}) custom-call(bf16[32,5120]{1,0:T(8,128)(2,1)} %get-tuple-element.11.dq, bf16[32,1024]{1,0:T(8,128)(2,1)} %get-tuple-element.12.dk, ...), custom_call_target="tpu_custom_call" | custom-call | tf_op jit(solution)/shard_map/finish/pallas_call | solution.py:555

commit v4 on v3

--- a/solution.py
+++ b/solution.py
@@ -21,13 +21,13 @@
 def coords():
     dp = lax.axis_index("dp")
     hd = lax.axis_index("head")
-    x, zl, y = lax.rem(dp, 4), lax.rem(dp // 4, 4), dp // 16
-    zh, c = hd // 2, lax.rem(hd, 2)
+    x, zl, y = lax.rem(dp, 4), lax.rem(lax.div(dp, 4), 4), lax.div(dp, 16)
+    zh, c = lax.div(hd, 2), lax.rem(hd, 2)
     return x, y, zh * 4 + zl, c
 
 
 def place(x, y, z, c):
-    return ((y * 4 + lax.rem(z, 4)) * 4 + x, (z // 4) * 2 + c)
+    return ((y * 4 + lax.rem(z, 4)) * 4 + x, lax.div(z, 4) * 2 + c)
 
 
 def wrap(a, n):
@@ -51,7 +51,7 @@
         self.s = 2 * self.x + self.c
         x, y, z, c, s = self.x, self.y, self.z, self.c, self.s
         self.group = [wrap(s + d, 8) for d in range(1, 8)]
-        self.group_dev = [place(g // 2, y, z, lax.rem(g, 2)) for g in self.group]
+        self.group_dev = [place(lax.div(g, 2), y, z, lax.rem(g, 2)) for g in self.group]
         self.sender = [wrap(s - d, 8) for d in range(1, 8)]
         self.y_dev = [place(x, wrap(y + d, 4), z, c) for d in range(1, 4)]
         self.z_near = [self.z_dev(k) for k in (1, -1, 2, -2)]
@@ -134,7 +134,7 @@
     pl.semaphore_wait(barrier, count)
 
     def masks():
-        zh = z // 4
+        zh = lax.div(z, 4)
         tab_s[4:8, :] = jnp.zeros((4, 256), jnp.int32)
         tab_row = tab_s[...].astype(F32)
         tab_col = tab_row.T
@@ -192,7 +192,7 @@
         part[n, :, 8:16, :] = dv.reshape(32, 8, D)
 
     def lead_grads():
-        p, zh = y * 4 + lax.rem(z, 4), z // 4
+        p, zh = y * 4 + lax.rem(z, 4), lax.div(z, 4)
         lead = pqd[...].astype(F32)
         q = stack([lead[:, i * 8 : i * 8 + 8, :].reshape(64, D) for i in range(QPK)]).astype(BF)
         do = stack([lead[:, (i + 5) * 8 : (i + 5) * 8 + 8, :].reshape(64, D) for i in range(QPK)]).astype(BF)
@@ -216,7 +216,7 @@
     def cols(ref, h, width):
         return ref.at[:, pl.ds(pl.multiple_of(h * width, D), width)]
 
-    mine = (y * 4 + lax.rem(z, 4), z // 4)
+    mine = (y * 4 + lax.rem(z, 4), lax.div(z, 4))
     sources = [
         lambda h: pkv_s.at[h],
         lambda h: cols(rk, h, D),
@@ -267,7 +267,7 @@
     send(3)
 
     def block(yy, zz):
-        return g_in.at[yy * 4 + lax.rem(zz, 4), zz // 4]
+        return g_in.at[yy * 4 + lax.rem(zz, 4), lax.div(zz, 4)]
 
     def moved(k):
         return block(y, wrap(z + k, 16))
@@ -375,13 +375,17 @@
         cur[1, two] = dv[576:640].reshape(2, 32, D)
         return 0
 
-    lax.fori_loop(0, 4, rank_grads, 0)
+    def two_ranks(r, _):
+        rank_grads(2 * r, 0)
+        return rank_grads(2 * r + 1, 0)
+
+    lax.fori_loop(0, 2, two_ranks, 0)
 
     owners = [prompts_of(jnp.int32(r)) for r in range(4)]
     part[9] = jnp.zeros((32, 16, D), F32)
 
     def summed(yy, zz):
-        p, rows = yy * 4 + lax.rem(zz, 4), pl.ds(zz // 4 * 8, 8)
+        p, rows = yy * 4 + lax.rem(zz, 4), pl.ds(lax.div(zz, 4) * 8, 8)
         total = None
         for r, (first, last) in enumerate(owners):
             n = jnp.where(first == p, 2 * r, jnp.where(last == p, 2 * r + 1, 9))
@@ -396,7 +400,7 @@
 
     def exchange(n, _):
         m = lax.rem(n, 4) + 1
-        zz = wrap(z + 4 * (n // 4 + 1) + m - 4 * (m // 3), 16)
+        zz = wrap(z + 4 * (lax.div(n, 4) + 1) + m - 4 * lax.div(m, 3), 16)
         for d in range(3):
             y_out[d, n] = summed(wrap(y + d + 1, 4), zz).astype(BF)
             y_copy(n, d).start()
@@ -444,7 +448,7 @@
     def partial(k, m):
         total = summed(y, at(k, m))
         if m == 3:
-            total += part[8, pl.ds(at(k, m) // 4 * 8, 8)]
+            total += part[8, pl.ds(lax.div(at(k, m), 4) * 8, 8)]
         for d in range(3):
             y_copy(4 * k + m, d).wait_recv()
             total += y_in[d, 4 * k + m].astype(F32)
@@ -535,7 +539,7 @@
             ((32, 40 * D), BF), ((32, 8 * D), BF), ((32, 8 * D), BF), ((8, 48, D), BF), ((8, 16, D), BF)
         ),
         in_specs=[pl.BlockSpec(memory_space=pl.ANY)] * 14,
-        out_specs=vmem(5),
+        out_specs=[pl.BlockSpec(memory_space=pl.ANY)] * 5,
         scratch_shapes=[
             bf(32, 40 * D), bf(32, 40 * D), bf(8, 40 * D), bf(8, 8 * D), bf(8, 8 * D), bf(8, 40 * D), bf(8, 40 * D),
             pltpu.VMEM((8, 256), jnp.int32), bf(8, 16, D), bf(8, 80, D), f32(8, 8, D),

time: 90.9 us -> 88.9 us (0.978)
  Pallas kernels: 90.1 us -> 87.7 us
    pallas_call x1, Pallas kernels: 88.2 us -> 85.8 us  [local(): pl.pallas_call(main_kernel, out_shape=shapes(((32, 40 * D), BF), ((32, 8...]
where the time goes in v4:
time: 88.9 us; the launch traced here: 88.3 us
  Pallas kernels  87.7 us (99%)
    pallas_call x1, Pallas kernels, local(): pl.pallas_call(main_kernel, out_shape=shapes(((32, 40 * D), BF), ((32, 8...  85.8 us
    pallas_call x1, Pallas kernels, local(): pl.pallas_call(finish_kernel, out_shape=shapes(((32, 40 * D), BF), ((32,...  1.87 us

profile of v4, /device:TPU:1, one launch (start us, length us, event | category | flops | bytes accessed | tf_op | source)
XLA Modules:
  0.0 88.3 jit_solution(16215788897606307906)
XLA Ops:
  0.6 85.8 %exchange_and_grads.1 = (bf16[32,5120]{1,0:T(8,128)(2,1)}, bf16[32,1024]{1,0:T(8,128)(2,1)}, bf16[32,1024]{1,0:T(8,128)(2,1)}, bf16[8,48,128]{2,1,0:T(8,128)(2,1)}, bf16[8,16,128]{2,1,0:T(8,128)(2,1)}) custom-call(bf16[32,5120]{1,0:T(8,128)(2,1)} %rq.1, bf16[32,1024]{1,0:T(8,128)(2,1)} %rk.1, bf16[32,1024]{1,0:T(8,128)(2,1)} %rv.1, bf16[32,5120]{1,0:T(8,128)(2,1)} %ro.1, ...), custom_call_target="tpu_custom_call" | custom-call | tf_op jit(solution)/shard_map/exchange_and_grads/pallas_call | solution.py:536
  86.5 1.9 %finish.1 = (bf16[32,5120]{1,0:T(8,128)(2,1)}, bf16[32,1024]{1,0:T(8,128)(2,1)}, bf16[32,1024]{1,0:T(8,128)(2,1)}, bf16[8,5120]{1,0:T(8,128)(2,1)}, bf16[8,1024]{1,0:T(8,128)(2,1)}, /*index=5*/bf16[8,1024]{1,0:T(8,128)(2,1)}) custom-call(bf16[32,5120]{1,0:T(8,128)(2,1)} %get-tuple-element.11.dq, bf16[32,1024]{1,0:T(8,128)(2,1)} %get-tuple-element.12.dk, ...), custom_call_target="tpu_custom_call" | custom-call | tf_op jit(solution)/shard_map/finish/pallas_call | solution.py:559
